TPU v7x, 32 devices: a whole 2x2x4 slice. The times are simulated.
32 devices in a mesh: groups: 2 (over y), ctx: 16 (over z, x, core).
Axes of the slice: x: 2, y: 2, z: 4, core: 2. Of those that a mesh axis runs over, the one named last changes fastest.
Arguments:
- query_vectors: bfloat16 [16384, 2048], P(('groups', 'ctx')), parts along dimension 0, may hold values from -60 to 60
- key_vectors: bfloat16 [16384, 2048], P(('groups', 'ctx')), parts along dimension 0, may hold values from -6 to 6
- value_vectors: bfloat16 [16384, 2048], P(('groups', 'ctx')), parts along dimension 0, may hold values from -8 to 8
- out_weight: bfloat16 [2048, 2048], P(None, 'ctx'), may hold values from -0.125 to 0.125
Outputs:
- projected: bfloat16 [16384, 2048], P(('groups', 'ctx')), parts along dimension 0
There are 2 independent parts, one for each index of `groups`. A program takes and returns all parts, laid end to end along the dimension named above; an argument that names none is the same for every part. Nothing has to cross between parts.
All inputs are finite; a program needn't handle non-finite values.
Results may differ from a plain program's by a relative error of at most 0.0095.
Values may be sent and summed in bfloat16 or wider, within the bound.
A program may use at most 192 MiB of HBM per device.

v0:
```python
import jax
import jax.numpy as jnp
from jax import lax
from jax.sharding import PartitionSpec as P

HEADS = 16
HEAD_DIM = 128
BLOCK = 128
LEVELS = 5


def shifted(block, axis, distance):
    devices = range(lax.axis_size(axis))
    route = [(i - distance, i) for i in devices if i - distance in devices]
    return lax.ppermute(block, axis, route)


def padded(block, sides, width):
    for axis, dim in sides:
        count = lax.axis_size(axis)
        forward = [(i, i + 1) for i in range(count - 1)]
        backward = [(target, source) for source, target in forward]
        low = lax.ppermute(
            lax.slice_in_dim(block, block.shape[dim] - width, None, axis=dim), axis, forward
        )
        high = lax.ppermute(lax.slice_in_dim(block, 0, width, axis=dim), axis, backward)
        block = jnp.concatenate([low, block, high], axis=dim)
    return block


def coarsen(matrix):
    paired = matrix.reshape(matrix.shape[0] // 2, 2, matrix.shape[1]).astype(jnp.float32)
    return ((paired[:, 0] + paired[:, 1]) * 0.5).astype(jnp.bfloat16)


def key_valid(height, block_index, row_pos, nblocks):
    grid_shape = (block_index.shape[0], row_pos.shape[0], BLOCK)
    has_left = jnp.broadcast_to((block_index >= 1)[:, None, None], grid_shape)
    has_right = jnp.broadcast_to((block_index + 1 < nblocks)[:, None, None], grid_shape)
    if height == 0:
        return jnp.concatenate([has_left, jnp.ones(grid_shape, jnp.bool_), has_right], axis=2)
    upper_half = (row_pos >= BLOCK // 2)[None, :, None]
    key_place = jnp.arange(BLOCK, dtype=jnp.int32)[None, None, :]
    left_ok = has_left & (upper_half | (key_place < BLOCK // 2))
    right_ok = has_right & (jnp.logical_not(upper_half) | (key_place >= BLOCK // 2))
    return jnp.concatenate([left_ok, right_ok], axis=2)


def attend(queries, keys_window, values_window, admitted):
    score_scale = HEAD_DIM ** (-0.5)
    mask_bias = jnp.where(admitted, 0.0, -jnp.inf).astype(jnp.float32)[:, None, :, :]
    scores = (
        jnp.einsum("nrhd,nkhd->nhrk", queries, keys_window, preferred_element_type=jnp.float32)
        * score_scale
        + mask_bias
    )
    row_peak = jnp.max(scores, axis=3)
    weights = jnp.exp(scores - row_peak[:, :, :, None]).astype(jnp.bfloat16)
    numerator = jnp.einsum(
        "nhrk,nkhd->nrhd", weights, values_window, preferred_element_type=jnp.float32
    )
    denominator = jnp.sum(weights.astype(jnp.float32), axis=3)
    return (jnp.transpose(row_peak, (0, 2, 1)), numerator, jnp.transpose(denominator, (0, 2, 1)))


def neighbour_blocks(key_value, span_devs, position):
    coarse_rows = key_value.shape[1]
    pieces = []
    for offset in range(1 - 2 * span_devs, 2 * span_devs):
        if offset == 0:
            pieces.append(key_value)
        else:
            pieces.append(shifted(key_value, "ctx", -offset))
    window = jnp.concatenate(pieces, axis=1)
    slice_start = (span_devs - 1 - position % span_devs) * coarse_rows
    left_keys = lax.dynamic_slice_in_dim(window, slice_start, BLOCK, 1)
    right_keys = lax.dynamic_slice_in_dim(window, slice_start + 2 * BLOCK, BLOCK, 1)
    return (left_keys, right_keys)


def merge_levels(peaks, numerators, denominators):
    spread = [jnp.repeat(peaks[height], 1 << height, axis=0) for height in range(len(peaks))]
    highest = spread[0]
    for level_peak in spread[1:]:
        highest = jnp.maximum(highest, level_peak)
    weighted = 0.0
    normaliser = 0.0
    for height in range(len(peaks)):
        factor = float(1 << height) * jnp.exp(spread[height] - highest)
        weighted = weighted + factor[:, :, None] * jnp.repeat(
            numerators[height], 1 << height, axis=0
        )
        normaliser = normaliser + factor * jnp.repeat(denominators[height], 1 << height, axis=0)
    return weighted / normaliser[:, :, None]


def per_device(query_vectors, key_vectors, value_vectors, out_weight):
    ctx_size = lax.axis_size("ctx")
    position = lax.axis_index("ctx")
    local_rows = query_vectors.shape[0]
    channels = query_vectors.shape[1]
    query_levels = [query_vectors]
    pair_levels = [jnp.stack([key_vectors, value_vectors])]
    for height in range(1, LEVELS):
        query_levels.append(coarsen(query_levels[-1]))
        previous = pair_levels[-1]
        pair_levels.append(jnp.stack([coarsen(previous[0]), coarsen(previous[1])]))
    local_levels = [height for height in range(LEVELS) if local_rows >> height >= BLOCK]
    rim_pairs = {}
    for height in local_levels:
        grown = padded(pair_levels[height], (("ctx", 1),), BLOCK)
        rim_pairs[height] = (grown[:, :BLOCK], grown[:, -BLOCK:])
    peaks, numerators, denominators = ([], [], [])
    for height in range(LEVELS):
        coarse_rows = local_rows >> height
        nblocks = local_rows * ctx_size // (BLOCK << height)
        key_value = pair_levels[height]
        if coarse_rows >= BLOCK:
            query_blocks = coarse_rows // BLOCK
            row_count = BLOCK
            left_rim, right_rim = rim_pairs[height]
            left_keys = jnp.concatenate([left_rim, key_value[:, : coarse_rows - BLOCK]], axis=1)
            right_keys = jnp.concatenate([key_value[:, BLOCK:], right_rim], axis=1)
            block_index = position * query_blocks + jnp.arange(query_blocks, dtype=jnp.int32)
            row_pos = jnp.arange(BLOCK, dtype=jnp.int32)
        else:
            span_devs = BLOCK // coarse_rows
            query_blocks = 1
            row_count = coarse_rows
            left_keys, right_keys = neighbour_blocks(key_value, span_devs, position)
            block_index = (position // span_devs)[None]
            row_pos = position % span_devs * coarse_rows + jnp.arange(coarse_rows, dtype=jnp.int32)
        grouped = (2, query_blocks, BLOCK, HEADS, HEAD_DIM)
        parts_list = [left_keys.reshape(grouped)]
        if height == 0:
            parts_list.append(key_value.reshape(grouped))
        parts_list.append(right_keys.reshape(grouped))
        window = jnp.concatenate(parts_list, axis=2)
        queries = query_levels[height].reshape(query_blocks, row_count, HEADS, HEAD_DIM)
        admitted = key_valid(height, block_index, row_pos, nblocks)
        row_peak, numerator, denominator = attend(queries, window[0], window[1], admitted)
        peaks.append(row_peak.reshape(coarse_rows, HEADS))
        numerators.append(numerator.reshape(coarse_rows, HEADS, HEAD_DIM))
        denominators.append(denominator.reshape(coarse_rows, HEADS))
    attended = (
        merge_levels(peaks, numerators, denominators)
        .astype(jnp.bfloat16)
        .reshape(local_rows, channels)
    )
    projected = jnp.dot(
        attended,
        lax.all_gather(out_weight, "ctx", axis=1, tiled=True),
        preferred_element_type=jnp.float32,
    )
    return projected.astype(jnp.bfloat16)


def solution(mesh):
    in_specs = (
        P(("groups", "ctx"), None),
        P(("groups", "ctx"), None),
        P(("groups", "ctx"), None),
        P(None, "ctx"),
    )
    out_specs = P(("groups", "ctx"), None)
    return jax.shard_map(
        per_device, mesh=mesh, in_specs=in_specs, out_specs=out_specs, check_vma=False
    )
```

profile of v0, /device:TPU:1, one launch (start us, length us, event | category | flops | bytes accessed | tf_op | source)
XLA Modules:
  0.0 533.8 jit_solution(1131327903527137976)
XLA Ops:
  6.5 5.4 %reshape.1190 = f32[256,2,2048]{2,1,0:T(2,128)} reshape(bf16[512,2048]{1,0:T(8,128)(2,1)} %param.5) | data formatting | bytes 6291456 | tf_op jit(solution)/shard_map/convert_element_type | solution.py:32
  12.0 13.1 %convert_reduce_fusion.3 = (f32[256,2048]{1,0:T(8,128)}, bf16[256,1,2048]{2,1,0:T(2,128)(2,1)}) fusion(f32[256,2,2048]{2,1,0:T(2,128)} %reshape.1190), kind=kLoop, calls=%fused_computation.60 | loop fusion | flops 2097152 | bytes 7340032 | tf_op jit(solution)/shard_map/convert_element_type | solution.py:32
  37.5 4.4 convert_reduce_fusion.9
  44.3 3.9 reshape.1191
  48.3 13.3 %convert_reduce_fusion.2 = (f32[256,2048]{1,0:T(8,128)}, bf16[256,1,2048]{2,1,0:T(2,128)(2,1)}) fusion(f32[256,2,2048]{2,1,0:T(2,128)} %reshape.1191), kind=kLoop, calls=%fused_computation.59 | loop fusion | flops 2097152 | bytes 7340032 | tf_op jit(solution)/shard_map/convert_element_type | solution.py:32
  65.0 5.7 %fusion.92 = (f32[128,1,2048]{2,1,0:T(1,128)}, f32[128,1,2048]{2,1,0:T(1,128)}) fusion(f32[128,2,2048]{2,1,0:T(2,128)} %reshape.1194), kind=kLoop, calls=%fused_computation.218 | loop fusion | bytes 4194304 | tf_op jit(solution)/shard_map/slice | solution.py:33
  83.6 4.4 convert_reduce_fusion.8
  98.4 7.5 %collective-permute-start.13 = (bf16[2,32,2048]{2,1,0:T(8,128)(2,1)}, bf16[2,32,2048]{2,1,0:T(8,128)(2,1)}, u32[]{:S(2)}, u32[]{:S(2)}) collective-permute-start(bf16[2,32,2048]{2,1,0:T(8,128)(2,1)} %pad_maximum_fusion.12), channel_id=1, source_target_pairs={{0,6},{1,7},{2,8},{3,9},{4,10},{5,11},{6,12},{7,13},{8,14},{9,15},... | collective-permute-start | bytes 786440 | tf_op jit(solution)/shard_map/ppermute | solution.py:15
  106.0 7.8 %collective-permute-start.12 = (bf16[2,32,2048]{2,1,0:T(8,128)(2,1)}, bf16[2,32,2048]{2,1,0:T(8,128)(2,1)}, u32[]{:S(2)}, u32[]{:S(2)}) collective-permute-start(bf16[2,32,2048]{2,1,0:T(8,128)(2,1)} %pad_maximum_fusion.12), channel_id=1, source_target_pairs={{0,7},{1,8},{2,9},{3,10},{4,11},{5,12},{6,13},{7,14},{8,15},{16,23... | collective-permute-start | bytes 786440 | tf_op jit(solution)/shard_map/ppermute | solution.py:15
  120.3 5.5 %reshape.1189 = f32[256,2,2048]{2,1,0:T(2,128)} reshape(bf16[512,2048]{1,0:T(8,128)(2,1)} %param.4) | data formatting | bytes 6291456 | tf_op jit(solution)/shard_map/convert_element_type | solution.py:32
  125.8 12.3 %convert_reduce_fusion.6 = (bf16[256,2048]{1,0:T(8,128)(2,1)}, bf16[256,1,2048]{2,1,0:T(2,128)(2,1)S(1)}) fusion(f32[256,2,2048]{2,1,0:T(2,128)} %reshape.1189), kind=kLoop, calls=%fused_computation.65 | loop fusion | flops 1572864 | bytes 6291456 | tf_op jit(solution)/shard_map/convert_element_type | solution.py:33
  138.1 7.3 %convert_reduce_fusion.4 = f32[256,2048]{1,0:T(8,128)} fusion(bf16[256,1,2048]{2,1,0:T(2,128)(2,1)S(1)} %get-tuple-element.12), kind=kLoop, calls=%fused_computation.61 | loop fusion | flops 524288 | bytes 3145728 | tf_op jit(solution)/shard_map/convert_element_type | solution.py:32
  148.8 5.7 %fusion.90 = (f32[128,1,2048]{2,1,0:T(1,128)}, f32[128,1,2048]{2,1,0:T(1,128)}) fusion(f32[128,2,2048]{2,1,0:T(2,128)} %reshape.1192), kind=kLoop, calls=%fused_computation.216 | loop fusion | bytes 4194304 | tf_op jit(solution)/shard_map/slice | solution.py:33
  158.1 3.8 copy.386
  167.6 4.3 convert_reduce_fusion.12
  181.0 3.7 copy_bitcast_fusion
  216.1 6.3 %collective-permute-start.18 = (bf16[2,32,2048]{2,1,0:T(8,128)(2,1)}, bf16[2,32,2048]{2,1,0:T(8,128)(2,1)S(1)}, u32[]{:S(2)}, u32[]{:S(2)}) collective-permute-start(bf16[2,32,2048]{2,1,0:T(8,128)(2,1)} %pad_maximum_fusion.12), channel_id=1, source_target_pairs={{0,1},{1,2},{2,3},{3,4},{4,5},{5,6},{6,7},{7,8},{8,9},{9,10},{10,1... | collective-permute-start | bytes 786440 | tf_op jit(solution)/shard_map/ppermute | solution.py:15
  227.9 8.9 %collective-permute-done.19 = bf16[2,32,2048]{2,1,0:T(8,128)(2,1)S(1)} collective-permute-done((bf16[2,32,2048]{2,1,0:T(8,128)(2,1)}, bf16[2,32,2048]{2,1,0:T(8,128)(2,1)S(1)}, u32[]{:S(2)}, u32[]{:S(2)}) %collective-permute-start.19) | collective-permute-done | bytes 262176 | tf_op jit(solution)/shard_map/ppermute | solution.py:15
  239.5 6.8 %collective-permute-done.21 = bf16[2,32,2048]{2,1,0:T(8,128)(2,1)S(1)} collective-permute-done((bf16[2,32,2048]{2,1,0:T(8,128)(2,1)}, bf16[2,32,2048]{2,1,0:T(8,128)(2,1)S(1)}, u32[]{:S(2)}, u32[]{:S(2)}) %collective-permute-start.21) | collective-permute-done | bytes 262176 | tf_op jit(solution)/shard_map/ppermute | solution.py:15
  247.6 7.2 %collective-permute-done.22 = bf16[2,32,2048]{2,1,0:T(8,128)(2,1)S(1)} collective-permute-done((bf16[2,32,2048]{2,1,0:T(8,128)(2,1)}, bf16[2,32,2048]{2,1,0:T(8,128)(2,1)S(1)}, u32[]{:S(2)}, u32[]{:S(2)}) %collective-permute-start.22) | collective-permute-done | bytes 262176 | tf_op jit(solution)/shard_map/ppermute | solution.py:15
  259.5 6.2 %collective-permute-start.7 = (bf16[2,64,2048]{2,1,0:T(8,128)(2,1)}, bf16[2,64,2048]{2,1,0:T(8,128)(2,1)}, u32[]{:S(2)}, u32[]{:S(2)}) collective-permute-start(bf16[2,64,2048]{2,1,0:T(8,128)(2,1)} %pad_maximum_fusion.11), channel_id=1, source_target_pairs={{0,2},{1,3},{2,4},{3,5},{4,6},{5,7},{6,8},{7,9},{8,10},{9,11},{10,... | collective-permute-start | bytes 1572872 | tf_op jit(solution)/shard_map/ppermute | solution.py:15
  282.3 15.8 %collective-permute-start.9 = (bf16[2,64,2048]{2,1,0:T(8,128)(2,1)}, bf16[2,64,2048]{2,1,0:T(8,128)(2,1)S(1)}, u32[]{:S(2)}, u32[]{:S(2)}) collective-permute-start(bf16[2,64,2048]{2,1,0:T(8,128)(2,1)} %pad_maximum_fusion.11), channel_id=1, source_target_pairs={{1,0},{2,1},{3,2},{4,3},{5,4},{6,5},{7,6},{8,7},{9,8},{10,9},{11,1... | collective-permute-start | bytes 1572872 | tf_op jit(solution)/shard_map/ppermute | solution.py:15
  309.3 4.5 collective-permute-start.2
  334.2 18.3 %collective-permute-done.4 = bf16[2,128,2048]{1,2,0:T(8,128)(2,1)} collective-permute-done((bf16[2,128,2048]{1,2,0:T(8,128)(2,1)}, bf16[2,128,2048]{1,2,0:T(8,128)(2,1)}, u32[]{:S(2)}, u32[]{:S(2)}) %collective-permute-start.4) | collective-permute-done | bytes 1048608 | tf_op jit(solution)/shard_map/ppermute | solution.py:23
  354.8 20.2 %collective-permute-done.2 = bf16[2,128,2048]{2,1,0:T(8,128)(2,1)} collective-permute-done((bf16[2,128,2048]{2,1,0:T(8,128)(2,1)}, bf16[2,128,2048]{2,1,0:T(8,128)(2,1)}, u32[]{:S(2)}, u32[]{:S(2)}) %collective-permute-start.2) | collective-permute-done | bytes 1048608 | tf_op jit(solution)/shard_map/ppermute | solution.py:23
  401.4 3.9 pad_maximum_fusion.1
  410.6 9.3 %pad_maximum_fusion = bf16[2,4,384,16,128]{4,2,3,1,0:T(8,128)(2,1)S(1)} fusion(bf16[2,4,128,16,128]{4,2,3,1,0:T(8,128)(2,1)S(1)} %copy.295, bf16[1,4,128,16,128]{4,2,3,1,0:T(8,128)(2,1)} %copy.293, bf16[1,4,128,16,128]{4,2,3,1,0:T(8,128)(2,1)} %copy.292, bf16[2,4,128,16,128]{4,2,3,1,0:T(8,128)(2,1)S(1)} %copy.294), kind=kLoop, calls=%fused_computation | loop fusion | flops 50331648 | bytes 25165824 | tf_op jit(solution)/shard_map/concatenate | solution.py:138
  419.9 6.0 %fusion = (f32[4,16,128]{2,1,0:T(8,128)S(1)}, f32[4,16,384,128]{3,2,1,0:T(8,128)}) fusion(f32[4,128,384]{1,2,0:T(8,128)S(1)} %add_select_fusion, bf16[4,128,16,128]{3,2,1,0:T(8,128)(2,1)S(1)} %bitcast.302, bf16[2,4,384,16,128]{4,2,3,1,0:T(8,128)(2,1)S(1)} %pad_maximum_fusion), kind=kOutput, calls=%fused_computation.4 | convolution fusion | flops 814735360 | bytes 21790720 | tf_op jit(solution)/shard_map/nrhd,nkhd->nhrk/dot_general | solution.py:53
  428.2 12.4 %fusion.11 = f32[4,128,16,128]{1,3,2,0:T(8,128)} fusion(bf16[2,4,384,16,128]{4,2,3,1,0:T(8,128)(2,1)} %copy-done, f32[4,16,384,128]{3,2,1,0:T(8,128)} %get-tuple-element.52, f32[4,16,128]{2,1,0:T(8,128)S(1)} %get-tuple-element.51, f32[4,128,384]{1,2,0:T(8,128)S(1)} %add_select_fusion), kind=kOutput, calls=%fused_computation.35 | convolution fusion | flops 817889280 | bytes 23887872 | tf_op jit(solution)/shard_map/nhrk,nkhd->nrhd/dot_general | solution.py:59
  440.6 5.4 %copy.341 = f32[4,128,16,128]{3,2,1,0:T(8,128)} copy(f32[4,128,16,128]{1,3,2,0:T(8,128)} %fusion.11) | data formatting | bytes 8388608 | tf_op jit(solution)/shard_map/nhrk,nkhd->nrhd/transpose | solution.py:59
  446.1 7.7 %convert_reduce_fusion = f32[4,16,128]{2,1,0:T(8,128)S(1)} fusion(f32[4,16,128]{2,1,0:T(8,128)S(1)} %get-tuple-element.51, f32[4,128,384]{1,2,0:T(8,128)S(1)} %add_select_fusion, f32[4,16,384,128]{3,2,1,0:T(8,128)} %get-tuple-element.52), kind=kLoop, calls=%fused_computation.2 | loop fusion | flops 18866176 | bytes 13434880 | tf_op jit(solution)/shard_map/reduce_sum | solution.py:62
  479.4 47.2 %convolution_convert_fusion = bf16[512,2048]{1,0:T(8,128)(2,1)} fusion(bf16[2048,2048]{1,0:T(8,128)(2,1)} %all-gather.2.cloned.1.call-done, f32[64,8,16,128]{3,2,1,0:T(8,128)} %bitcast.324, f32[64,8,16,128]{3,2,1,0:T(8,128)} %bitcast.318, f32[64,8,16,128]{3,2,1,0:T(8,128)} %bitcast.320, f32[64,8,16,128]{3,2,1,0:T(8,128)} %bitcast.321, ...), kind=kOutput, calls=%fused_computation.34 | convolution fusion | flops 4307550208 | bytes 52953088 | tf_op jit(solution)/shard_map/dot_general | solution.py:150
  (278 shorter events, 224.2 us)
Async XLA Ops:
  6.5 448.9 %all-gather.2.cloned.1.call-start = ((), (), s32[]{:S(2)}) async-start(), calls=%async_computation | async-start | bytes 8912896 | tf_op jit(solution)/shard_map/all_gather | solution.py:152
  79.6 12.3 %copy-start.11 = (bf16[128,1,2048]{0,2,1:T(8,128)(2,1)}, bf16[128,1,2048]{0,2,1:T(8,128)(2,1)S(1)}, u32[]{:S(2)}) copy-start(bf16[128,1,2048]{0,2,1:T(8,128)(2,1)S(1)} %multiply_convert_fusion) | copy-start | bytes 1572868
  94.6 172.1 %collective-permute-start.25 = (bf16[2,32,2048]{2,1,0:T(8,128)(2,1)}, bf16[2,32,2048]{2,1,0:T(8,128)(2,1)}, u32[]{:S(2)}, u32[]{:S(2)}) collective-permute-start(bf16[2,32,2048]{2,1,0:T(8,128)(2,1)} %pad_maximum_fusion.12), channel_id=1, source_target_pairs={{7,0},{8,1},{9,2},{10,3},{11,4},{12,5},{13,6},{14,7},{15,8},{23,16... | collective-permute-start | bytes 786440 | tf_op jit(solution)/shard_map/ppermute | solution.py:15
  95.8 163.6 %collective-permute-start.24 = (bf16[2,32,2048]{2,1,0:T(8,128)(2,1)}, bf16[2,32,2048]{2,1,0:T(8,128)(2,1)}, u32[]{:S(2)}, u32[]{:S(2)}) collective-permute-start(bf16[2,32,2048]{2,1,0:T(8,128)(2,1)} %pad_maximum_fusion.12), channel_id=1, source_target_pairs={{6,0},{7,1},{8,2},{9,3},{10,4},{11,5},{12,6},{13,7},{14,8},{15,9},... | collective-permute-start | bytes 786440 | tf_op jit(solution)/shard_map/ppermute | solution.py:15
  97.1 159.0 %collective-permute-start.23 = (bf16[2,32,2048]{2,1,0:T(8,128)(2,1)}, bf16[2,32,2048]{2,1,0:T(8,128)(2,1)}, u32[]{:S(2)}, u32[]{:S(2)}) collective-permute-start(bf16[2,32,2048]{2,1,0:T(8,128)(2,1)} %pad_maximum_fusion.12), channel_id=1, source_target_pairs={{5,0},{6,1},{7,2},{8,3},{9,4},{10,5},{11,6},{12,7},{13,8},{14,9},{... | collective-permute-start | bytes 786440 | tf_op jit(solution)/shard_map/ppermute | solution.py:15
  98.4 103.8 %collective-permute-start.13 = (bf16[2,32,2048]{2,1,0:T(8,128)(2,1)}, bf16[2,32,2048]{2,1,0:T(8,128)(2,1)}, u32[]{:S(2)}, u32[]{:S(2)}) collective-permute-start(bf16[2,32,2048]{2,1,0:T(8,128)(2,1)} %pad_maximum_fusion.12), channel_id=1, source_target_pairs={{0,6},{1,7},{2,8},{3,9},{4,10},{5,11},{6,12},{7,13},{8,14},{9,15},... | collective-permute-start | bytes 786440 | tf_op jit(solution)/shard_map/ppermute | solution.py:15
  106.0 94.0 %collective-permute-start.12 = (bf16[2,32,2048]{2,1,0:T(8,128)(2,1)}, bf16[2,32,2048]{2,1,0:T(8,128)(2,1)}, u32[]{:S(2)}, u32[]{:S(2)}) collective-permute-start(bf16[2,32,2048]{2,1,0:T(8,128)(2,1)} %pad_maximum_fusion.12), channel_id=1, source_target_pairs={{0,7},{1,8},{2,9},{3,10},{4,11},{5,12},{6,13},{7,14},{8,15},{16,23... | collective-permute-start | bytes 786440 | tf_op jit(solution)/shard_map/ppermute | solution.py:15
  198.1 29.8 %copy-start.25 = (bf16[1,32,2048]{2,1,0:T(8,128)(2,1)S(1)}, bf16[1,32,2048]{2,1,0:T(8,128)(2,1)}, u32[]{:S(2)}) copy-start(bf16[1,32,2048]{2,1,0:T(8,128)(2,1)} %copy-done.24) | copy-start | bytes 393220
  198.1 29.8 %copy-start.27 = (bf16[1,32,2048]{2,1,0:T(8,128)(2,1)S(1)}, bf16[1,32,2048]{2,1,0:T(8,128)(2,1)}, u32[]{:S(2)}) copy-start(bf16[1,32,2048]{2,1,0:T(8,128)(2,1)} %copy-done.26) | copy-start | bytes 393220
  200.0 7.7 %collective-permute-start.14 = (bf16[2,32,2048]{2,1,0:T(8,128)(2,1)}, bf16[2,32,2048]{2,1,0:T(8,128)(2,1)S(1)}, u32[]{:S(2)}, u32[]{:S(2)}) collective-permute-start(bf16[2,32,2048]{2,1,0:T(8,128)(2,1)} %pad_maximum_fusion.12), channel_id=1, source_target_pairs={{0,5},{1,6},{2,7},{3,8},{4,9},{5,10},{6,11},{7,12},{8,13},{9,14},{... | collective-permute-start | bytes 786440 | tf_op jit(solution)/shard_map/ppermute | solution.py:15
  202.3 10.4 %collective-permute-start.15 = (bf16[2,32,2048]{2,1,0:T(8,128)(2,1)}, bf16[2,32,2048]{2,1,0:T(8,128)(2,1)S(1)}, u32[]{:S(2)}, u32[]{:S(2)}) collective-permute-start(bf16[2,32,2048]{2,1,0:T(8,128)(2,1)} %pad_maximum_fusion.12), channel_id=1, source_target_pairs={{0,4},{1,5},{2,6},{3,7},{4,8},{5,9},{6,10},{7,11},{8,12},{9,13},{1... | collective-permute-start | bytes 786440 | tf_op jit(solution)/shard_map/ppermute | solution.py:15
  207.6 8.4 %collective-permute-start.16 = (bf16[2,32,2048]{2,1,0:T(8,128)(2,1)}, bf16[2,32,2048]{2,1,0:T(8,128)(2,1)S(1)}, u32[]{:S(2)}, u32[]{:S(2)}) collective-permute-start(bf16[2,32,2048]{2,1,0:T(8,128)(2,1)} %pad_maximum_fusion.12), channel_id=1, source_target_pairs={{0,3},{1,4},{2,5},{3,6},{4,7},{5,8},{6,9},{7,10},{8,11},{9,12},{10... | collective-permute-start | bytes 786440 | tf_op jit(solution)/shard_map/ppermute | solution.py:15
  212.7 9.7 %collective-permute-start.17 = (bf16[2,32,2048]{2,1,0:T(8,128)(2,1)}, bf16[2,32,2048]{2,1,0:T(8,128)(2,1)S(1)}, u32[]{:S(2)}, u32[]{:S(2)}) collective-permute-start(bf16[2,32,2048]{2,1,0:T(8,128)(2,1)} %pad_maximum_fusion.12), channel_id=1, source_target_pairs={{0,2},{1,3},{2,4},{3,5},{4,6},{5,7},{6,8},{7,9},{8,10},{9,11},{10,... | collective-permute-start | bytes 786440 | tf_op jit(solution)/shard_map/ppermute | solution.py:15
  216.1 9.9 %collective-permute-start.18 = (bf16[2,32,2048]{2,1,0:T(8,128)(2,1)}, bf16[2,32,2048]{2,1,0:T(8,128)(2,1)S(1)}, u32[]{:S(2)}, u32[]{:S(2)}) collective-permute-start(bf16[2,32,2048]{2,1,0:T(8,128)(2,1)} %pad_maximum_fusion.12), channel_id=1, source_target_pairs={{0,1},{1,2},{2,3},{3,4},{4,5},{5,6},{6,7},{7,8},{8,9},{9,10},{10,1... | collective-permute-start | bytes 786440 | tf_op jit(solution)/shard_map/ppermute | solution.py:15
  222.4 15.8 %collective-permute-start.20 = (bf16[2,32,2048]{2,1,0:T(8,128)(2,1)}, bf16[2,32,2048]{2,1,0:T(8,128)(2,1)S(1)}, u32[]{:S(2)}, u32[]{:S(2)}) collective-permute-start(bf16[2,32,2048]{2,1,0:T(8,128)(2,1)} %pad_maximum_fusion.12), channel_id=1, source_target_pairs={{2,0},{3,1},{4,2},{5,3},{6,4},{7,5},{8,6},{9,7},{10,8},{11,9},{12,... | collective-permute-start | bytes 786440 | tf_op jit(solution)/shard_map/ppermute | solution.py:15
  225.9 10.9 %collective-permute-start.19 = (bf16[2,32,2048]{2,1,0:T(8,128)(2,1)}, bf16[2,32,2048]{2,1,0:T(8,128)(2,1)S(1)}, u32[]{:S(2)}, u32[]{:S(2)}) collective-permute-start(bf16[2,32,2048]{2,1,0:T(8,128)(2,1)} %pad_maximum_fusion.12), channel_id=1, source_target_pairs={{1,0},{2,1},{3,2},{4,3},{5,4},{6,5},{7,6},{8,7},{9,8},{10,9},{11,1... | collective-permute-start | bytes 786440 | tf_op jit(solution)/shard_map/ppermute | solution.py:15
  236.8 9.5 %collective-permute-start.21 = (bf16[2,32,2048]{2,1,0:T(8,128)(2,1)}, bf16[2,32,2048]{2,1,0:T(8,128)(2,1)S(1)}, u32[]{:S(2)}, u32[]{:S(2)}) collective-permute-start(bf16[2,32,2048]{2,1,0:T(8,128)(2,1)} %pad_maximum_fusion.12), channel_id=1, source_target_pairs={{3,0},{4,1},{5,2},{6,3},{7,4},{8,5},{9,6},{10,7},{11,8},{12,9},{13... | collective-permute-start | bytes 786440 | tf_op jit(solution)/shard_map/ppermute | solution.py:15
  238.2 16.7 %collective-permute-start.22 = (bf16[2,32,2048]{2,1,0:T(8,128)(2,1)}, bf16[2,32,2048]{2,1,0:T(8,128)(2,1)S(1)}, u32[]{:S(2)}, u32[]{:S(2)}) collective-permute-start(bf16[2,32,2048]{2,1,0:T(8,128)(2,1)} %pad_maximum_fusion.12), channel_id=1, source_target_pairs={{4,0},{5,1},{6,2},{7,3},{8,4},{9,5},{10,6},{11,7},{12,8},{13,9},{1... | collective-permute-start | bytes 786440 | tf_op jit(solution)/shard_map/ppermute | solution.py:15
  246.3 68.6 %collective-permute-start.11 = (bf16[2,64,2048]{2,1,0:T(8,128)(2,1)}, bf16[2,64,2048]{2,1,0:T(8,128)(2,1)}, u32[]{:S(2)}, u32[]{:S(2)}) collective-permute-start(bf16[2,64,2048]{2,1,0:T(8,128)(2,1)} %pad_maximum_fusion.11), channel_id=1, source_target_pairs={{3,0},{4,1},{5,2},{6,3},{7,4},{8,5},{9,6},{10,7},{11,8},{12,9},{13... | collective-permute-start | bytes 1572872 | tf_op jit(solution)/shard_map/ppermute | solution.py:15
  254.8 54.4 %collective-permute-start.10 = (bf16[2,64,2048]{2,1,0:T(8,128)(2,1)}, bf16[2,64,2048]{2,1,0:T(8,128)(2,1)}, u32[]{:S(2)}, u32[]{:S(2)}) collective-permute-start(bf16[2,64,2048]{2,1,0:T(8,128)(2,1)} %pad_maximum_fusion.11), channel_id=1, source_target_pairs={{2,0},{3,1},{4,2},{5,3},{6,4},{7,5},{8,6},{9,7},{10,8},{11,9},{12,... | collective-permute-start | bytes 1572872 | tf_op jit(solution)/shard_map/ppermute | solution.py:15
  256.1 46.2 %collective-permute-start.8 = (bf16[2,64,2048]{2,1,0:T(8,128)(2,1)}, bf16[2,64,2048]{2,1,0:T(8,128)(2,1)}, u32[]{:S(2)}, u32[]{:S(2)}) collective-permute-start(bf16[2,64,2048]{2,1,0:T(8,128)(2,1)} %pad_maximum_fusion.11), channel_id=1, source_target_pairs={{0,1},{1,2},{2,3},{3,4},{4,5},{5,6},{6,7},{7,8},{8,9},{9,10},{10,1... | collective-permute-start | bytes 1572872 | tf_op jit(solution)/shard_map/ppermute | solution.py:15
  259.5 39.8 %collective-permute-start.7 = (bf16[2,64,2048]{2,1,0:T(8,128)(2,1)}, bf16[2,64,2048]{2,1,0:T(8,128)(2,1)}, u32[]{:S(2)}, u32[]{:S(2)}) collective-permute-start(bf16[2,64,2048]{2,1,0:T(8,128)(2,1)} %pad_maximum_fusion.11), channel_id=1, source_target_pairs={{0,2},{1,3},{2,4},{3,5},{4,6},{5,7},{6,8},{7,9},{8,10},{9,11},{10,... | collective-permute-start | bytes 1572872 | tf_op jit(solution)/shard_map/ppermute | solution.py:15
  266.7 15.7 %collective-permute-start.6 = (bf16[2,64,2048]{2,1,0:T(8,128)(2,1)}, bf16[2,64,2048]{2,1,0:T(8,128)(2,1)}, u32[]{:S(2)}, u32[]{:S(2)}) collective-permute-start(bf16[2,64,2048]{2,1,0:T(8,128)(2,1)} %pad_maximum_fusion.11), channel_id=1, source_target_pairs={{0,3},{1,4},{2,5},{3,6},{4,7},{5,8},{6,9},{7,10},{8,11},{9,12},{10... | collective-permute-start | bytes 1572872 | tf_op jit(solution)/shard_map/ppermute | solution.py:15
  278.0 29.0 %copy-start.19 = (bf16[1,64,2048]{2,1,0:T(8,128)(2,1)S(1)}, bf16[1,64,2048]{2,1,0:T(8,128)(2,1)}, u32[]{:S(2)}) copy-start(bf16[1,64,2048]{2,1,0:T(8,128)(2,1)} %copy-done.18) | copy-start | bytes 786436
  278.0 29.0 %copy-start.21 = (bf16[1,64,2048]{2,1,0:T(8,128)(2,1)S(1)}, bf16[1,64,2048]{2,1,0:T(8,128)(2,1)}, u32[]{:S(2)}) copy-start(bf16[1,64,2048]{2,1,0:T(8,128)(2,1)} %copy-done.20) | copy-start | bytes 786436
  282.3 24.8 %collective-permute-start.9 = (bf16[2,64,2048]{2,1,0:T(8,128)(2,1)}, bf16[2,64,2048]{2,1,0:T(8,128)(2,1)S(1)}, u32[]{:S(2)}, u32[]{:S(2)}) collective-permute-start(bf16[2,64,2048]{2,1,0:T(8,128)(2,1)} %pad_maximum_fusion.11), channel_id=1, source_target_pairs={{1,0},{2,1},{3,2},{4,3},{5,4},{6,5},{7,6},{8,7},{9,8},{10,9},{11,1... | collective-permute-start | bytes 1572872 | tf_op jit(solution)/shard_map/ppermute | solution.py:15
  299.3 30.7 %collective-permute-start.5 = (bf16[2,128,2048]{1,2,0:T(8,128)(2,1)}, bf16[2,128,2048]{1,2,0:T(8,128)(2,1)}, u32[]{:S(2)}, u32[]{:S(2)}) collective-permute-start(bf16[2,128,2048]{1,2,0:T(8,128)(2,1)} %pad_maximum_fusion.10), channel_id=1, source_target_pairs={{1,0},{2,1},{3,2},{4,3},{5,4},{6,5},{7,6},{8,7},{9,8},{10,9},{11,1... | collective-permute-start | bytes 3145736 | tf_op jit(solution)/shard_map/ppermute | solution.py:26
  302.3 50.2 %collective-permute-start.4 = (bf16[2,128,2048]{1,2,0:T(8,128)(2,1)}, bf16[2,128,2048]{1,2,0:T(8,128)(2,1)}, u32[]{:S(2)}, u32[]{:S(2)}) collective-permute-start(bf16[2,128,2048]{1,2,0:T(8,128)(2,1)} %pad_maximum_fusion.10), channel_id=1, source_target_pairs={{0,1},{1,2},{2,3},{3,4},{4,5},{5,6},{6,7},{7,8},{8,9},{9,10},{10,1... | collective-permute-start | bytes 3145736 | tf_op jit(solution)/shard_map/ppermute | solution.py:23
  307.1 94.3 %collective-permute-start = (bf16[2,128,2048]{2,1,0:T(8,128)(2,1)}, bf16[2,128,2048]{2,1,0:T(8,128)(2,1)}, u32[]{:S(2)}, u32[]{:S(2)}) collective-permute-start(bf16[2,128,2048]{2,1,0:T(8,128)(2,1)} %get-tuple-element.23), channel_id=1, source_target_pairs={{0,1},{1,2},{2,3},{3,4},{4,5},{5,6},{6,7},{7,8},{8,9},{9,10},{10,1... | collective-permute-start | bytes 3145736 | tf_op jit(solution)/shard_map/ppermute | solution.py:23
  309.3 65.7 %collective-permute-start.2 = (bf16[2,128,2048]{2,1,0:T(8,128)(2,1)}, bf16[2,128,2048]{2,1,0:T(8,128)(2,1)}, u32[]{:S(2)}, u32[]{:S(2)}) collective-permute-start(bf16[2,128,2048]{2,1,0:T(8,128)(2,1)} %get-tuple-element.31), channel_id=1, source_target_pairs={{0,1},{1,2},{2,3},{3,4},{4,5},{5,6},{6,7},{7,8},{8,9},{9,10},{10,1... | collective-permute-start | bytes 3145736 | tf_op jit(solution)/shard_map/ppermute | solution.py:23
  314.9 63.9 %collective-permute-start.3 = (bf16[2,128,2048]{2,1,0:T(8,128)(2,1)}, bf16[2,128,2048]{2,1,0:T(8,128)(2,1)}, u32[]{:S(2)}, u32[]{:S(2)}) collective-permute-start(bf16[2,128,2048]{2,1,0:T(8,128)(2,1)} %get-tuple-element.32), channel_id=1, source_target_pairs={{1,0},{2,1},{3,2},{4,3},{5,4},{6,5},{7,6},{8,7},{9,8},{10,9},{11,1... | collective-permute-start | bytes 3145736 | tf_op jit(solution)/shard_map/ppermute | solution.py:26
  329.9 71.4 %collective-permute-start.1 = (bf16[2,128,2048]{2,1,0:T(8,128)(2,1)}, bf16[2,128,2048]{2,1,0:T(8,128)(2,1)}, u32[]{:S(2)}, u32[]{:S(2)}) collective-permute-start(bf16[2,128,2048]{2,1,0:T(8,128)(2,1)} %get-tuple-element.24), channel_id=1, source_target_pairs={{1,0},{2,1},{3,2},{4,3},{5,4},{6,5},{7,6},{8,7},{9,8},{10,9},{11,1... | collective-permute-start | bytes 3145736 | tf_op jit(solution)/shard_map/ppermute | solution.py:26
  (31 other events, 130.5 us)
Sparse Core Ops, SparseCore 0:
  114.0 84.1 all-gather.1
where the time goes:
time: 545 us; the launch traced here: 534 us
  local copies, waits for them, and re-layouts  178 us (33%)
  other arithmetic  111 us (20%)
  starting transfers between devices  84.3 us (15%)
  matrix products  75.7 us (14%)
  waiting for transfers between devices  70.5 us (13%)
  between operations  15 us (3%)
    ppermute x20, starting transfers between devices, shifted(): return lax.ppermute(block, axis, route)  68.3 us
    unnamed x108, local copies, waits for them, and re-layouts  47.9 us
    dot_general x1, matrix products, per_device(): jnp.dot(attended, lax.all_gather(out_weight, 'ctx', axis=1, tiled=True),...  47.2 us
    convert_element_type x6, other arithmetic, coarsen(): matrix.reshape(matrix.shape[0] // 2, 2, matrix.shape[1]).astype(jnp.float32)  44.8 us
    convert_element_type x15, local copies, waits for them, and re-layouts, coarsen(): matrix.reshape(matrix.shape[0] // 2, 2, matrix.shape[1]).astype(jnp.float32)  42 us
    ppermute x3, waiting for transfers between devices, padded(): lax.ppermute(lax.slice_in_dim(block, block.shape[dim] - width, None, axis...  38.5 us
    ppermute x20, waiting for transfers between devices, shifted(): return lax.ppermute(block, axis, route)  31.9 us
    convert_element_type x6, other arithmetic, coarsen(): return ((paired[:, 0] + paired[:, 1]) * 0.5).astype(jnp.bfloat16)  21.3 us
  transfers between devices with their start and end apart: 27, of which 8 were waited for; matrix products, arithmetic and copies ran while one was open for 38% of the time, Pallas kernels for 0%

commit v1 on v0

v1 whole, which is shorter than its diff:
```python
import functools
import math

import jax
import jax.numpy as jnp
from jax import lax
from jax.experimental import pallas as pl
from jax.experimental.pallas import tpu as pltpu
from jax.sharding import PartitionSpec as P

HEADS = 16
HEAD_DIM = 128
BLOCK = 128
HALF = BLOCK // 2
BF16 = jnp.bfloat16
F32 = jnp.float32
RATE = HEAD_DIM ** (-0.5) * math.log2(math.e)
MASKED = -1e30


def pool(rows):
    count = rows.shape[0] // 2
    at = lax.broadcasted_iota(jnp.int32, (count, 2 * count), 0)
    source = lax.broadcasted_iota(jnp.int32, (count, 2 * count), 1)
    half = jnp.where((source >> 1) == at, 0.5, 0.0).astype(BF16)
    return jnp.dot(half, rows, preferred_element_type=F32).astype(BF16)


def messages_kernel(k_ref, v_ref, right_ref, left_ref, third_ref, fourth_ref):
    for which, ref in enumerate((k_ref, v_ref)):
        rows = ref[...]
        first = pool(rows)
        second = pool(first)
        third = pool(second)
        right_ref[which, 0:128] = rows[384:512]
        right_ref[which, 128:192] = first[128:192]
        right_ref[which, 192:256] = second[0:64]
        left_ref[which, 0:128] = rows[0:128]
        left_ref[which, 128:192] = first[64:128]
        left_ref[which, 192:256] = second[64:128]
        third_ref[which] = third
        fourth_ref[which] = pool(third)


def make_messages(keys, values):
    width = keys.shape[1]
    cols = 512
    shapes = [256, 256, 64, 32]
    return pl.pallas_call(
        messages_kernel,
        grid=(width // cols,),
        in_specs=[pl.BlockSpec((512, cols), lambda j: (0, j))] * 2,
        out_specs=[pl.BlockSpec((2, n, cols), lambda j: (0, 0, j)) for n in shapes],
        out_shape=[jax.ShapeDtypeStruct((2, n, width), BF16) for n in shapes],
        compiler_params=pltpu.CompilerParams(vmem_limit_bytes=40 << 20),
        name="messages",
    )(keys, values)


def attend(queries, keys, values, bias=None):
    scores = lax.dot_general(queries, keys, (((1,), (1,)), ((), ())), preferred_element_type=F32)
    if bias is not None:
        scores = scores + bias
    peak = jnp.max(scores, axis=1, keepdims=True)
    weights = jnp.exp2((scores - peak) * RATE).astype(BF16)
    ones = jnp.ones((values.shape[0], HEAD_DIM), BF16)
    both = jnp.dot(weights, jnp.concatenate([values, ones], axis=1), preferred_element_type=F32)
    return (
        jnp.broadcast_to(peak, (queries.shape[0], HEAD_DIM)),
        both[:, :HEAD_DIM],
        both[:, HEAD_DIM:],
    )


def stack(parts):
    return tuple(jnp.concatenate(items, axis=0) for items in zip(*parts))


def merged(height, fine, coarse, scratch):
    rows = fine[0].shape[0]
    spread = []
    for which, part in enumerate(coarse):
        scratch[which, pl.ds(0, rows // 2, stride=2), :] = part
        scratch[which, pl.ds(1, rows // 2, stride=2), :] = part
        spread.append(scratch[which, pl.ds(0, rows), :])
    top = jnp.maximum(fine[0], spread[0])
    here = jnp.exp2((fine[0] - top) * RATE) * float(1 << height)
    there = jnp.exp2((spread[0] - top) * RATE)
    return (top, here * fine[1] + there * spread[1], here * fine[2] + there * spread[2])


def bias_row(pieces):
    total = sum(count for count, _ in pieces)
    lane = lax.broadcasted_iota(jnp.int32, (1, total), 1)
    row = jnp.zeros((1, total), F32)
    start = 0
    for count, allowed in pieces:
        if allowed is not None:
            inside = (lane >= start) & (lane < start + count)
            row = jnp.where(inside, jnp.where(allowed, 0.0, MASKED), row)
        start += count
    return row


def edge_flags(height, position, ctx_size):
    span = max(1, (1 << height) // 4)
    block = position // span
    return block >= 1, block + 1 < ctx_size // span


def head_attention(position, ctx_size, q, kv, left, right, thirds, fourths, scratch):
    k_of = lambda x: x[:, :HEAD_DIM]
    v_of = lambda x: x[:, HEAD_DIM:]
    everything = jnp.concatenate([kv, q], axis=1)
    levels = [everything]
    for _ in range(4):
        levels.append(pool(levels[-1]))
    q_at = [level[:, 2 * HEAD_DIM :] for level in levels]
    kv_at = [level[:, : 2 * HEAD_DIM] for level in levels]

    left0, left1b = left[0:128], left[128:192]
    right0, right1b = right[0:128], right[128:192]
    left1 = jnp.concatenate([left1b, pool(left0)], axis=0)
    right1 = jnp.concatenate([pool(right0), right1b], axis=0)
    left2 = jnp.concatenate([left[192:256], pool(left1)], axis=0)
    right2 = jnp.concatenate([pool(right1), right[192:256]], axis=0)

    def window(queries, pieces):
        rows = jnp.concatenate([piece for piece, _ in pieces], axis=0)
        bias = None
        if any(allowed is not None for _, allowed in pieces):
            bias = bias_row([(piece.shape[0], allowed) for piece, allowed in pieces])
        return attend(queries, k_of(rows), v_of(rows), bias)

    def halves(queries, before, has_before, after, has_after):
        return [
            window(queries[:HALF], [(before[:HALF], has_before), (after, has_after)]),
            window(queries[HALF:], [(before, has_before), (after[HALF:], has_after)]),
        ]

    has_left, has_right = edge_flags(4, position, ctx_size)
    turn = position % 4
    tests = [has_left, has_right]
    from_right = [
        (turn == 1) | (turn == 3),
        (turn == 0) | (turn == 2),
        (turn == 0) | (turn == 1),
        (turn == 0) | (turn == 1),
    ]
    pieces = [(fourths[0], has_left), (fourths[1], has_right)]
    for chunk, is_right in zip(fourths[2:], from_right):
        pieces.append((chunk, (is_right & has_right) | (~is_right & has_left)))
    peak, total, weight = window(q_at[4], pieces)
    state = (peak, total * 16.0, weight * 16.0)

    has_left, has_right = edge_flags(3, position, ctx_size)
    is_right = position % 2 == 0
    mixed = (is_right & has_right) | (~is_right & has_left)
    state = merged(
        3,
        window(
            q_at[3], [(thirds[0], has_left), (thirds[1], has_right), (thirds[2], mixed)]
        ),
        state,
        scratch,
    )

    has_left, has_right = edge_flags(2, position, ctx_size)
    state = merged(2, stack(halves(q_at[2], left2, has_left, right2, has_right)), state, scratch)

    kv1 = kv_at[1]
    state = merged(
        1,
        stack(
            halves(q_at[1][:128], left1, has_left, kv1[128:], None)
            + halves(q_at[1][128:], kv1[:128], None, right1, has_right)
        ),
        state,
        scratch,
    )

    parts = [window(q[0:128], [(left0, has_left), (kv[0:256], None)])]
    for block in (1, 2):
        start = 128 * block
        parts.append(window(q[start : start + 128], [(kv[start - 128 : start + 256], None)]))
    parts.append(window(q[384:512], [(kv[256:512], None), (right0, has_right)]))
    _, total, weight = merged(0, stack(parts), state, scratch)
    return (total / weight).astype(BF16)


def attention_kernel(ctx_size, pos_ref, q_ref, k_ref, v_ref, left_ref, right_ref, *rest):
    chunks, out_ref, scratch = rest[:9], rest[9], rest[10]
    pair = lambda ref: jnp.concatenate([ref[0], ref[1]], axis=1)
    kv = jnp.concatenate([k_ref[...], v_ref[...]], axis=1)
    chunk_rows = [pair(ref) for ref in chunks]
    out_ref[...] = head_attention(
        pos_ref[0],
        ctx_size,
        q_ref[...],
        kv,
        pair(left_ref),
        pair(right_ref),
        chunk_rows[:3],
        chunk_rows[3:],
        scratch,
    )


def attention(ctx_size, position, queries, keys, values, left, right, thirds, fourths):
    rows, width = queries.shape
    own = pl.BlockSpec((rows, HEAD_DIM), lambda h: (0, h))
    beside = lambda n: pl.BlockSpec((2, n, HEAD_DIM), lambda h: (0, 0, h))
    return pl.pallas_call(
        functools.partial(attention_kernel, ctx_size),
        grid=(HEADS,),
        in_specs=[pl.BlockSpec(memory_space=pltpu.SMEM), own, own, own, beside(256), beside(256)]
        + [beside(64)] * 3
        + [beside(32)] * 6,
        out_specs=own,
        out_shape=jax.ShapeDtypeStruct((rows, width), BF16),
        scratch_shapes=[pltpu.VMEM((3, rows, HEAD_DIM), F32)],
        compiler_params=pltpu.CompilerParams(vmem_limit_bytes=40 << 20),
        name="attention",
    )(position[None].astype(jnp.int32), queries, keys, values, left, right, *thirds, *fourths)


def project_kernel(x_ref, w_ref, out_ref):
    weight = jnp.concatenate([w_ref[0], w_ref[1]], axis=1)
    out_ref[...] = jnp.dot(x_ref[...], weight, preferred_element_type=F32).astype(BF16)


def project(attended, shards):
    rows, width = attended.shape
    count, _, cols = shards.shape
    return pl.pallas_call(
        project_kernel,
        grid=(count // 2,),
        in_specs=[
            pl.BlockSpec((rows, width), lambda j: (0, 0)),
            pl.BlockSpec((2, width, cols), lambda j: (j, 0, 0)),
        ],
        out_specs=pl.BlockSpec((rows, 2 * cols), lambda j: (0, j)),
        out_shape=jax.ShapeDtypeStruct((rows, count * cols), BF16),
        compiler_params=pltpu.CompilerParams(vmem_limit_bytes=40 << 20),
        name="project",
    )(attended, shards)


def moved(array, ctx_size, offset_of):
    route = []
    for target in range(ctx_size):
        source = target + offset_of(target)
        if 0 <= source < ctx_size:
            route.append((source, target))
    return lax.ppermute(array, "ctx", route)


THIRD_OFFSETS = [lambda i: -2, lambda i: 2, lambda i: (3, -3)[i % 2]]
FOURTH_OFFSETS = [
    lambda i: -4,
    lambda i: 4,
    lambda i: (-3, 3, -3, 3)[i % 4],
    lambda i: (5, -5, 5, -5)[i % 4],
    lambda i: (6, 6, -6, -6)[i % 4],
    lambda i: (7, 5, -5, -7)[i % 4],
]


def per_device(query_vectors, key_vectors, value_vectors, out_weight):
    ctx_size = lax.axis_size("ctx")
    position = lax.axis_index("ctx")
    whole_shards = out_weight.shape[1] % 128 == 0
    if whole_shards:
        weight = lax.all_gather(out_weight, "ctx", axis=0)
    else:
        weight = lax.all_gather(out_weight, "ctx", axis=1, tiled=True)
    to_right, to_left, third, fourth = make_messages(key_vectors, value_vectors)
    left = moved(to_right, ctx_size, lambda i: -1)
    right = moved(to_left, ctx_size, lambda i: 1)
    thirds = [moved(third, ctx_size, offset) for offset in THIRD_OFFSETS]
    fourths = [moved(fourth, ctx_size, offset) for offset in FOURTH_OFFSETS]
    attended = attention(
        ctx_size, position, query_vectors, key_vectors, value_vectors, left, right, thirds, fourths
    )
    if whole_shards:
        return project(attended, weight)
    return jnp.dot(attended, weight, preferred_element_type=F32).astype(BF16)


def solution(mesh):
    in_specs = (
        P(("groups", "ctx"), None),
        P(("groups", "ctx"), None),
        P(("groups", "ctx"), None),
        P(None, "ctx"),
    )
    out_specs = P(("groups", "ctx"), None)
    return jax.shard_map(
        per_device, mesh=mesh, in_specs=in_specs, out_specs=out_specs, check_vma=False
    )
```

time: 545 us -> 227 us (0.42)
  the two profiles are of different devices: /device:TPU:1 before, /device:TPU:8 now
where the time goes in v1:
time: 227 us; the launch traced here: 226 us
  waiting for transfers between devices  84.8 us (37%)
  Pallas kernels  72.1 us (32%)
  starting transfers between devices  34.9 us (15%)
  local copies, waits for them, and re-layouts  20.9 us (9%)
  between operations  13.6 us (6%)
    ppermute x11, waiting for transfers between devices, moved(): return lax.ppermute(array, 'ctx', route)  84.1 us
    pallas_call x1, Pallas kernels, attention(): pl.pallas_call(functools.partial(attention_kernel, ctx_size), grid=(HEADS...  59.1 us
    ppermute x11, starting transfers between devices, moved(): return lax.ppermute(array, 'ctx', route)  34.9 us
    unnamed x36, local copies, waits for them, and re-layouts  20.9 us
    pallas_call x1, Pallas kernels, make_messages(): pl.pallas_call(messages_kernel, grid=(width // cols,), in_specs=[pl.Block...  6.57 us
    pallas_call x1, Pallas kernels, project(): pl.pallas_call(project_kernel, grid=(count // 2,), in_specs=[pl.BlockSpec...  6.51 us
  transfers between devices with their start and end apart: 12, of which 7 were waited for; matrix products, arithmetic and copies ran while one was open for 0% of the time, Pallas kernels for 29%

profile of v1, /device:TPU:8, one launch (start us, length us, event | category | flops | bytes accessed | tf_op | source)
XLA Modules:
  0.0 226.2 jit_solution(236283857052338036)
XLA Ops:
  7.3 1.6 copy-done
  8.9 1.6 copy-done.2
  10.4 6.6 %messages.1 = (bf16[2,256,2048]{2,1,0:T(8,128)(2,1)}, bf16[2,256,2048]{2,1,0:T(8,128)(2,1)}, bf16[2,64,2048]{2,1,0:T(8,128)(2,1)}, bf16[2,32,2048]{2,1,0:T(8,128)(2,1)S(1)}) custom-call(bf16[512,2048]{1,0:T(8,128)(2,1)S(1)} %copy-done, bf16[512,2048]{1,0:T(8,128)(2,1)S(1)} %copy-done.2), custom_call_target="tpu_custom_call" | custom-call | tf_op jit(solution)/shard_map/messages/pallas_call | solution.py:49
  17.0 1.9 collective-permute-start
  18.9 4.5 %collective-permute-start.1 = (bf16[2,256,2048]{2,1,0:T(8,128)(2,1)}, bf16[2,256,2048]{2,1,0:T(8,128)(2,1)}, u32[]{:S(2)}, u32[]{:S(2)}) collective-permute-start(bf16[2,256,2048]{2,1,0:T(8,128)(2,1)} %get-tuple-element.10), channel_id=1, source_target_pairs={{1,0},{2,1},{3,2},{4,3},{5,4},{6,5},{7,6},{8,7},{9,8},{10,9},{11,1... | collective-permute-start | bytes 6291464 | tf_op jit(solution)/shard_map/ppermute | solution.py:255
  23.5 3.0 %collective-permute-start.10 = (bf16[2,32,2048]{2,1,0:T(8,128)(2,1)S(1)}, bf16[2,32,2048]{2,1,0:T(8,128)(2,1)S(1)}, u32[]{:S(2)}, u32[]{:S(2)}) collective-permute-start(bf16[2,32,2048]{2,1,0:T(8,128)(2,1)S(1)} %get-tuple-element.12), channel_id=1, source_target_pairs={{7,0},{6,1},{11,4},{10,5},{1,6},{0,7},{15,8},{14,9},{5,10},{4,11},... | collective-permute-start | bytes 786440 | tf_op jit(solution)/shard_map/ppermute | solution.py:255
  26.5 3.7 %collective-permute-start.5 = (bf16[2,32,2048]{2,1,0:T(8,128)(2,1)S(1)}, bf16[2,32,2048]{2,1,0:T(8,128)(2,1)S(1)}, u32[]{:S(2)}, u32[]{:S(2)}) collective-permute-start(bf16[2,32,2048]{2,1,0:T(8,128)(2,1)S(1)} %get-tuple-element.12), channel_id=1, source_target_pairs={{0,4},{1,5},{2,6},{3,7},{4,8},{5,9},{6,10},{7,11},{8,12},{9,13},{1... | collective-permute-start | bytes 786440 | tf_op jit(solution)/shard_map/ppermute | solution.py:255
  30.2 2.2 collective-permute-start.6
  32.4 11.0 %collective-permute-done.10.rest_8_ = bf16[2,32,2048]{2,1,0:T(8,128)(2,1)S(1)} collective-permute-done((bf16[2,32,2048]{2,1,0:T(8,128)(2,1)S(1)}, bf16[2,32,2048]{2,1,0:T(8,128)(2,1)S(1)}, u32[]{:S(2)}, u32[]{:S(2)}) %collective-permute-start.10) | collective-permute-done | bytes 262176 | tf_op jit(solution)/shard_map/ppermute | solution.py:255
  43.4 3.7 %collective-permute-start.7 = (bf16[2,32,2048]{2,1,0:T(8,128)(2,1)S(1)}, bf16[2,32,2048]{2,1,0:T(8,128)(2,1)S(1)}, u32[]{:S(2)}, u32[]{:S(2)}) collective-permute-start(bf16[2,32,2048]{2,1,0:T(8,128)(2,1)S(1)} %get-tuple-element.12), channel_id=1, source_target_pairs={{4,1},{6,3},{1,4},{8,5},{3,6},{10,7},{5,8},{12,9},{7,10},{14,11},{... | collective-permute-start | bytes 786440 | tf_op jit(solution)/shard_map/ppermute | solution.py:255
  47.1 1.6 collective-permute-done.5.rest_3_
  49.4 3.1 %collective-permute-start.8 = (bf16[2,32,2048]{2,1,0:T(8,128)(2,1)S(1)}, bf16[2,32,2048]{2,1,0:T(8,128)(2,1)S(1)}, u32[]{:S(2)}, u32[]{:S(2)}) collective-permute-start(bf16[2,32,2048]{2,1,0:T(8,128)(2,1)S(1)} %get-tuple-element.12), channel_id=1, source_target_pairs={{5,0},{7,2},{9,4},{0,5},{11,6},{2,7},{13,8},{4,9},{15,10},{6,11},{... | collective-permute-start | bytes 786440 | tf_op jit(solution)/shard_map/ppermute | solution.py:255
  52.6 36.8 %collective-permute-done.6.rest_4_ = bf16[2,32,2048]{2,1,0:T(8,128)(2,1)S(1)} collective-permute-done((bf16[2,32,2048]{2,1,0:T(8,128)(2,1)S(1)}, bf16[2,32,2048]{2,1,0:T(8,128)(2,1)S(1)}, u32[]{:S(2)}, u32[]{:S(2)}) %collective-permute-start.6) | collective-permute-done | bytes 262176 | tf_op jit(solution)/shard_map/ppermute | solution.py:255
  90.1 4.0 %collective-permute-start.9 = (bf16[2,32,2048]{2,1,0:T(8,128)(2,1)S(1)}, bf16[2,32,2048]{2,1,0:T(8,128)(2,1)S(1)}, u32[]{:S(2)}, u32[]{:S(2)}) collective-permute-start(bf16[2,32,2048]{2,1,0:T(8,128)(2,1)S(1)} %get-tuple-element.12), channel_id=1, source_target_pairs={{6,0},{7,1},{10,4},{11,5},{0,6},{1,7},{14,8},{15,9},{4,10},{5,11},... | collective-permute-start | bytes 786440 | tf_op jit(solution)/shard_map/ppermute | solution.py:255
  94.8 1.9 collective-permute-start.2
  97.4 4.8 %collective-permute-start.3 = (bf16[2,64,2048]{2,1,0:T(8,128)(2,1)}, bf16[2,64,2048]{2,1,0:T(8,128)(2,1)S(1)}, u32[]{:S(2)}, u32[]{:S(2)}) collective-permute-start(bf16[2,64,2048]{2,1,0:T(8,128)(2,1)} %get-tuple-element.11), channel_id=1, source_target_pairs={{2,0},{3,1},{4,2},{5,3},{6,4},{7,5},{8,6},{9,7},{10,8},{11,9},{12,... | collective-permute-start | bytes 1572872 | tf_op jit(solution)/shard_map/ppermute | solution.py:255
  102.3 1.1 collective-permute-done.9.rest_7_
  104.0 1.9 collective-permute-start.4
  106.0 24.5 %collective-permute-done.2.rest_0_ = bf16[2,64,2048]{2,1,0:T(8,128)(2,1)S(1)} collective-permute-done((bf16[2,64,2048]{2,1,0:T(8,128)(2,1)}, bf16[2,64,2048]{2,1,0:T(8,128)(2,1)S(1)}, u32[]{:S(2)}, u32[]{:S(2)}) %collective-permute-start.2) | collective-permute-done | bytes 524320 | tf_op jit(solution)/shard_map/ppermute | solution.py:255
  130.5 6.4 %collective-permute-done.3.rest_1_ = bf16[2,64,2048]{2,1,0:T(8,128)(2,1)S(1)} collective-permute-done((bf16[2,64,2048]{2,1,0:T(8,128)(2,1)}, bf16[2,64,2048]{2,1,0:T(8,128)(2,1)S(1)}, u32[]{:S(2)}, u32[]{:S(2)}) %collective-permute-start.3) | collective-permute-done | bytes 524320 | tf_op jit(solution)/shard_map/ppermute | solution.py:255
  136.8 2.7 %collective-permute-done.4.rest_2_ = bf16[2,64,2048]{2,1,0:T(8,128)(2,1)} collective-permute-done((bf16[2,64,2048]{2,1,0:T(8,128)(2,1)}, bf16[2,64,2048]{2,1,0:T(8,128)(2,1)}, u32[]{:S(2)}, u32[]{:S(2)}) %collective-permute-start.4) | collective-permute-done | bytes 524320 | tf_op jit(solution)/shard_map/ppermute | solution.py:255
  139.6 1.6 copy-done.3
  141.2 1.6 copy-done.7
  142.8 0.9 copy-done.9
  143.7 0.9 copy-done.11
  144.7 0.9 copy-done.13
  146.6 0.9 copy-done.17
  147.5 59.1 %attention.1.x_ref = bf16[512,2048]{1,0:T(8,128)(2,1)S(1)} custom-call(s32[1]{0:T(128)} %bitcast.pos_ref, bf16[512,2048]{1,0:T(8,128)(2,1)S(1)} %copy-done.7, bf16[512,2048]{1,0:T(8,128)(2,1)S(1)} %copy-done.1, bf16[512,2048]{1,0:T(8,128)(2,1)S(1)} %copy-done.3, bf16[2,256,2048]{2,1,0:T(8,128)(2,1)} %collective-permute-done.left_ref, ...), custom_call_target="tpu_custom_call" | custom-call | tf_op jit(solution)/shard_map/attention/pallas_call | solution.py:213
  206.6 1.3 copy-done.5
  207.9 3.4 %copy-done.4 = bf16[32768,128]{1,0:T(8,128)(2,1)S(1)} copy-done((bf16[32768,128]{1,0:T(8,128)(2,1)S(1)}, bf16[32768,128]{1,0:T(8,128)(2,1)}, u32[]{:S(2)}) %copy-start.4) | copy-done | bytes 8388632
  211.3 1.6 copy-done.6
  212.9 6.5 %project.1 = bf16[512,2048]{1,0:T(8,128)(2,1)} custom-call(bf16[512,2048]{1,0:T(8,128)(2,1)S(1)} %copy-done.6, bf16[16,2048,128]{2,1,0:T(8,128)(2,1)S(1)} %bitcast.2), custom_call_target="tpu_custom_call" | custom-call | tf_op jit(solution)/shard_map/project/pallas_call | solution.py:235
  (32 shorter events, 5.2 us)
Async XLA Ops:
  6.5 201.4 %all-gather.3.cloned.1.call-start = ((), (), s32[]{:S(2)}) async-start(), calls=%async_computation | async-start | bytes 8912896 | tf_op jit(solution)/shard_map/all_gather | solution.py:274
  7.3 1.6 copy-start
  8.8 1.6 copy-start.2
  10.4 129.1 %copy-start.1 = (bf16[512,2048]{1,0:T(8,128)(2,1)S(1)}, bf16[512,2048]{1,0:T(8,128)(2,1)}, u32[]{:S(2)}) copy-start(bf16[512,2048]{1,0:T(8,128)(2,1)} %k_ref.3) | copy-start | bytes 6291460
  17.0 122.6 %collective-permute-start = (bf16[2,256,2048]{2,1,0:T(8,128)(2,1)}, bf16[2,256,2048]{2,1,0:T(8,128)(2,1)}, u32[]{:S(2)}, u32[]{:S(2)}) collective-permute-start(bf16[2,256,2048]{2,1,0:T(8,128)(2,1)} %get-tuple-element.9), channel_id=1, source_target_pairs={{0,1},{1,2},{2,3},{3,4},{4,5},{5,6},{6,7},{7,8},{8,9},{9,10},{10,1... | collective-permute-start | bytes 6291464 | tf_op jit(solution)/shard_map/ppermute | solution.py:255
  18.9 120.7 %collective-permute-start.1 = (bf16[2,256,2048]{2,1,0:T(8,128)(2,1)}, bf16[2,256,2048]{2,1,0:T(8,128)(2,1)}, u32[]{:S(2)}, u32[]{:S(2)}) collective-permute-start(bf16[2,256,2048]{2,1,0:T(8,128)(2,1)} %get-tuple-element.10), channel_id=1, source_target_pairs={{1,0},{2,1},{3,2},{4,3},{5,4},{6,5},{7,6},{8,7},{9,8},{10,9},{11,1... | collective-permute-start | bytes 6291464 | tf_op jit(solution)/shard_map/ppermute | solution.py:255
  23.5 19.9 %collective-permute-start.10 = (bf16[2,32,2048]{2,1,0:T(8,128)(2,1)S(1)}, bf16[2,32,2048]{2,1,0:T(8,128)(2,1)S(1)}, u32[]{:S(2)}, u32[]{:S(2)}) collective-permute-start(bf16[2,32,2048]{2,1,0:T(8,128)(2,1)S(1)} %get-tuple-element.12), channel_id=1, source_target_pairs={{7,0},{6,1},{11,4},{10,5},{1,6},{0,7},{15,8},{14,9},{5,10},{4,11},... | collective-permute-start | bytes 786440 | tf_op jit(solution)/shard_map/ppermute | solution.py:255
  26.5 22.2 %collective-permute-start.5 = (bf16[2,32,2048]{2,1,0:T(8,128)(2,1)S(1)}, bf16[2,32,2048]{2,1,0:T(8,128)(2,1)S(1)}, u32[]{:S(2)}, u32[]{:S(2)}) collective-permute-start(bf16[2,32,2048]{2,1,0:T(8,128)(2,1)S(1)} %get-tuple-element.12), channel_id=1, source_target_pairs={{0,4},{1,5},{2,6},{3,7},{4,8},{5,9},{6,10},{7,11},{8,12},{9,13},{1... | collective-permute-start | bytes 786440 | tf_op jit(solution)/shard_map/ppermute | solution.py:255
  30.2 59.1 %collective-permute-start.6 = (bf16[2,32,2048]{2,1,0:T(8,128)(2,1)S(1)}, bf16[2,32,2048]{2,1,0:T(8,128)(2,1)S(1)}, u32[]{:S(2)}, u32[]{:S(2)}) collective-permute-start(bf16[2,32,2048]{2,1,0:T(8,128)(2,1)S(1)} %get-tuple-element.12), channel_id=1, source_target_pairs={{4,0},{5,1},{6,2},{7,3},{8,4},{9,5},{10,6},{11,7},{12,8},{13,9},{1... | collective-permute-start | bytes 786440 | tf_op jit(solution)/shard_map/ppermute | solution.py:255
  43.4 50.7 %collective-permute-start.7 = (bf16[2,32,2048]{2,1,0:T(8,128)(2,1)S(1)}, bf16[2,32,2048]{2,1,0:T(8,128)(2,1)S(1)}, u32[]{:S(2)}, u32[]{:S(2)}) collective-permute-start(bf16[2,32,2048]{2,1,0:T(8,128)(2,1)S(1)} %get-tuple-element.12), channel_id=1, source_target_pairs={{4,1},{6,3},{1,4},{8,5},{3,6},{10,7},{5,8},{12,9},{7,10},{14,11},{... | collective-permute-start | bytes 786440 | tf_op jit(solution)/shard_map/ppermute | solution.py:255
  48.7 0.7 copy-start.8
  49.4 47.3 %collective-permute-start.8 = (bf16[2,32,2048]{2,1,0:T(8,128)(2,1)S(1)}, bf16[2,32,2048]{2,1,0:T(8,128)(2,1)S(1)}, u32[]{:S(2)}, u32[]{:S(2)}) collective-permute-start(bf16[2,32,2048]{2,1,0:T(8,128)(2,1)S(1)} %get-tuple-element.12), channel_id=1, source_target_pairs={{5,0},{7,2},{9,4},{0,5},{11,6},{2,7},{13,8},{4,9},{15,10},{6,11},{... | collective-permute-start | bytes 786440 | tf_op jit(solution)/shard_map/ppermute | solution.py:255
  89.3 0.7 copy-start.10
  90.1 13.3 %collective-permute-start.9 = (bf16[2,32,2048]{2,1,0:T(8,128)(2,1)S(1)}, bf16[2,32,2048]{2,1,0:T(8,128)(2,1)S(1)}, u32[]{:S(2)}, u32[]{:S(2)}) collective-permute-start(bf16[2,32,2048]{2,1,0:T(8,128)(2,1)S(1)} %get-tuple-element.12), channel_id=1, source_target_pairs={{6,0},{7,1},{10,4},{11,5},{0,6},{1,7},{14,8},{15,9},{4,10},{5,11},... | collective-permute-start | bytes 786440 | tf_op jit(solution)/shard_map/ppermute | solution.py:255
  94.1 0.7 copy-start.12
  94.8 35.7 %collective-permute-start.2 = (bf16[2,64,2048]{2,1,0:T(8,128)(2,1)}, bf16[2,64,2048]{2,1,0:T(8,128)(2,1)S(1)}, u32[]{:S(2)}, u32[]{:S(2)}) collective-permute-start(bf16[2,64,2048]{2,1,0:T(8,128)(2,1)} %get-tuple-element.11), channel_id=1, source_target_pairs={{0,2},{1,3},{2,4},{3,5},{4,6},{5,7},{6,8},{7,9},{8,10},{9,11},{10,... | collective-permute-start | bytes 1572872 | tf_op jit(solution)/shard_map/ppermute | solution.py:255
  96.8 0.7 copy-start.14
  97.4 39.4 %collective-permute-start.3 = (bf16[2,64,2048]{2,1,0:T(8,128)(2,1)}, bf16[2,64,2048]{2,1,0:T(8,128)(2,1)S(1)}, u32[]{:S(2)}, u32[]{:S(2)}) collective-permute-start(bf16[2,64,2048]{2,1,0:T(8,128)(2,1)} %get-tuple-element.11), channel_id=1, source_target_pairs={{2,0},{3,1},{4,2},{5,3},{6,4},{7,5},{8,6},{9,7},{10,8},{11,9},{12,... | collective-permute-start | bytes 1572872 | tf_op jit(solution)/shard_map/ppermute | solution.py:255
  103.3 0.7 copy-start.16
  104.0 35.5 %collective-permute-start.4 = (bf16[2,64,2048]{2,1,0:T(8,128)(2,1)}, bf16[2,64,2048]{2,1,0:T(8,128)(2,1)}, u32[]{:S(2)}, u32[]{:S(2)}) collective-permute-start(bf16[2,64,2048]{2,1,0:T(8,128)(2,1)} %get-tuple-element.11), channel_id=1, source_target_pairs={{3,0},{5,2},{0,3},{7,4},{2,5},{9,6},{4,7},{11,8},{6,9},{13,10},{8,... | collective-permute-start | bytes 1572872 | tf_op jit(solution)/shard_map/ppermute | solution.py:255
  139.6 1.6 copy-start.3
  141.2 1.6 copy-start.7
  142.8 0.9 copy-start.9
  143.7 0.9 copy-start.11
  144.7 0.9 copy-start.13
  145.6 0.9 copy-start.15
  146.6 0.9 copy-start.17
  206.6 1.3 copy-start.5
  207.9 3.4 %copy-start.4 = (bf16[32768,128]{1,0:T(8,128)(2,1)S(1)}, bf16[32768,128]{1,0:T(8,128)(2,1)}, u32[]{:S(2)}) copy-start(bf16[32768,128]{1,0:T(8,128)(2,1)} %all-gather.3.cloned.1.call-done) | copy-start | bytes 25165828
  211.3 1.6 copy-start.6
Sparse Core Ops, SparseCore 0:
  9.5 112.8 all-gather.2

commit v2 on v1

--- a/solution.py
+++ b/solution.py
@@ -24,37 +24,6 @@
     source = lax.broadcasted_iota(jnp.int32, (count, 2 * count), 1)
     half = jnp.where((source >> 1) == at, 0.5, 0.0).astype(BF16)
     return jnp.dot(half, rows, preferred_element_type=F32).astype(BF16)
-
-
-def messages_kernel(k_ref, v_ref, right_ref, left_ref, third_ref, fourth_ref):
-    for which, ref in enumerate((k_ref, v_ref)):
-        rows = ref[...]
-        first = pool(rows)
-        second = pool(first)
-        third = pool(second)
-        right_ref[which, 0:128] = rows[384:512]
-        right_ref[which, 128:192] = first[128:192]
-        right_ref[which, 192:256] = second[0:64]
-        left_ref[which, 0:128] = rows[0:128]
-        left_ref[which, 128:192] = first[64:128]
-        left_ref[which, 192:256] = second[64:128]
-        third_ref[which] = third
-        fourth_ref[which] = pool(third)
-
-
-def make_messages(keys, values):
-    width = keys.shape[1]
-    cols = 512
-    shapes = [256, 256, 64, 32]
-    return pl.pallas_call(
-        messages_kernel,
-        grid=(width // cols,),
-        in_specs=[pl.BlockSpec((512, cols), lambda j: (0, j))] * 2,
-        out_specs=[pl.BlockSpec((2, n, cols), lambda j: (0, 0, j)) for n in shapes],
-        out_shape=[jax.ShapeDtypeStruct((2, n, width), BF16) for n in shapes],
-        compiler_params=pltpu.CompilerParams(vmem_limit_bytes=40 << 20),
-        name="messages",
-    )(keys, values)
 
 
 def attend(queries, keys, values, bias=None):
@@ -188,102 +157,330 @@
     return (total / weight).astype(BF16)
 
 
-def attention_kernel(ctx_size, pos_ref, q_ref, k_ref, v_ref, left_ref, right_ref, *rest):
-    chunks, out_ref, scratch = rest[:9], rest[9], rest[10]
-    pair = lambda ref: jnp.concatenate([ref[0], ref[1]], axis=1)
-    kv = jnp.concatenate([k_ref[...], v_ref[...]], axis=1)
-    chunk_rows = [pair(ref) for ref in chunks]
-    out_ref[...] = head_attention(
-        pos_ref[0],
-        ctx_size,
-        q_ref[...],
-        kv,
-        pair(left_ref),
-        pair(right_ref),
-        chunk_rows[:3],
-        chunk_rows[3:],
-        scratch,
-    )
-
-
-def attention(ctx_size, position, queries, keys, values, left, right, thirds, fourths):
+SLOT_OFFSETS = [
+    (-1, -1, -1, -1),
+    (1, 1, 1, 1),
+    (-2, -2, -2, -2),
+    (2, 2, 2, 2),
+    (3, -3, 3, -3),
+    (-4, -4, -4, -4),
+    (4, 4, 4, 4),
+    (-3, 3, -3, 3),
+    (5, -5, 5, -5),
+    (6, 6, -6, -6),
+    (7, 5, -5, -7),
+]
+REACH = 7
+CHUNKS = 8
+CHUNK_HEADS = HEADS // CHUNKS
+
+
+def by_turn(turn, table):
+    value = table[3]
+    for at in (2, 1, 0):
+        value = jnp.where(turn == at, table[at], value)
+    return value
+
+
+def inverse(table):
+    back = [0, 0, 0, 0]
+    for turn, offset in enumerate(table):
+        back[(turn + offset) % 4] = -offset
+    return tuple(back)
+
+
+def layer_kernel(ctx_size, with_weight, *refs):
+    if with_weight:
+        q_ref, k_ref, v_ref, w_ref, out_ref = refs[:5]
+        refs = refs[5:]
+        w_all, w_recv, w_send, w_core = refs[-4:]
+    else:
+        q_ref, k_ref, v_ref, out_ref = refs[:4]
+        refs = refs[4:]
+    (to_right, to_left, third, fourth, left, right, thirds, fourths,
+     scratch, att, send_sem, recv_sem) = refs[:12]
+
+    position = lax.axis_index("ctx")
+    group = lax.axis_index("groups")
+    turn = position % 4
+
+    barrier = pltpu.get_barrier_semaphore()
+    reach = ctx_size - 1 if with_weight else min(REACH, ctx_size - 1)
+    for distance in range(1, reach + 1):
+        for offset in (-distance, distance):
+            peer = position + offset
+
+            @pl.when((peer >= 0) & (peer < ctx_size))
+            def _():
+                pl.semaphore_signal(
+                    barrier, inc=1, device_id={"ctx": peer}, device_id_type=pl.DeviceIdType.MESH
+                )
+
+    peers = jnp.minimum(position, reach) + jnp.minimum(ctx_size - 1 - position, reach)
+    if with_weight:
+        pl.semaphore_signal(
+            barrier, inc=1, device_id={"groups": 1 - group}, device_id_type=pl.DeviceIdType.MESH
+        )
+        peers = peers + 1
+
+    slots = [left, right] + [thirds.at[i] for i in range(3)] + [fourths.at[i] for i in range(6)]
+    sources = [to_right, to_left] + [third] * 3 + [fourth] * 6
+    givers = [position + by_turn(turn, table) for table in SLOT_OFFSETS]
+    takers = [position + by_turn(turn, inverse(table)) for table in SLOT_OFFSETS]
+    inside = lambda peer: (peer >= 0) & (peer < ctx_size)
+
+    pl.semaphore_wait(barrier, peers)
+
+    for slot, giver in zip(slots, givers):
+
+        @pl.when(jnp.logical_not(inside(giver)))
+        def _():
+            slot[...] = jnp.zeros(slot.shape, BF16)
+
+    def slot_copy(chunk, which):
+        heads = pl.ds(chunk * CHUNK_HEADS, CHUNK_HEADS)
+        return pltpu.make_async_remote_copy(
+            src_ref=sources[which].at[heads],
+            dst_ref=slots[which].at[heads],
+            send_sem=send_sem.at[chunk, which],
+            recv_sem=recv_sem.at[chunk, which],
+            device_id={"ctx": takers[which]},
+            device_id_type=pl.DeviceIdType.MESH,
+        )
+
+    steps = []
+    if with_weight:
+        z = position // 4
+        depth = ctx_size // 4
+        partner = position + 2 - 4 * ((position // 2) % 2)
+        sibling = position + 1 - 2 * (position % 2)
+
+        def piece(shard, half, send, device):
+            return pltpu.make_async_remote_copy(
+                src_ref=w_all.at[shard, half],
+                dst_ref=w_all.at[shard, half],
+                send_sem=send,
+                recv_sem=w_recv.at[shard, half],
+                device_id=device,
+                device_id_type=pl.DeviceIdType.MESH,
+            )
+
+        def to_x(shard):
+            return piece(shard, group, w_send.at[0, shard], {"ctx": partner})
+
+        def to_z(shard, way):
+            kind = 1 if way > 0 else 2
+            return piece(shard, group, w_send.at[kind, shard], {"ctx": position + 4 * way})
+
+        def to_y(shard):
+            return piece(shard, group, w_send.at[3, shard], {"groups": 1 - group})
+
+        def to_core(shard, half, own):
+            send = w_send.at[4, shard] if own else w_core.at[shard]
+            return piece(shard, half, send, {"ctx": sibling})
+
+        always = None
+        can_go = {1: z + 1 < depth, -1: z >= 1}
+        first = [(always, lambda: to_x(position))]
+        for way in (1, -1):
+            first.append((can_go[way], functools.partial(to_z, position, way)))
+        first.append((always, lambda: to_core(position, group, True)))
+        first.append((always, lambda: to_core(position, 1 - group, False)))
+        steps.append([(always, None, first)])
+        second = [(can_go[way], functools.partial(to_z, partner, way)) for way in (1, -1)]
+        second.append((always, lambda: to_y(partner)))
+        second.append((always, lambda: to_core(partner, group, True)))
+        steps.append([(always, (partner, group), second)])
+        for hops in range(1, depth):
+            step = []
+            for way in (1, -1):
+                here = (z - hops * way >= 0) & (z - hops * way < depth)
+                for base in (position, partner):
+                    shard = base - 4 * hops * way
+                    sends = [
+                        (can_go[way], functools.partial(to_z, shard, way)),
+                        (always, functools.partial(to_y, shard)),
+                        (always, functools.partial(to_core, shard, group, True)),
+                    ]
+                    step.append((here, (shard, group), sends))
+            steps.append(step)
+        step = []
+        for turns in range(depth):
+            for base in (position, partner):
+                if turns == 0 and base is position:
+                    continue
+                level = lax.rem(z + turns, depth)
+                shard = base + 4 * (level - z)
+                sends = [(always, functools.partial(to_core, shard, 1 - group, False))]
+                step.append((always, (shard, 1 - group), sends))
+        steps.append(step)
+
+    def when(condition, action):
+        if condition is None:
+            action()
+        else:
+            pl.when(condition)(action)
+
+    def run_step(step):
+        for here, awaited, sends in step:
+
+            def act(awaited=awaited, sends=sends):
+                if awaited is not None:
+                    piece(*awaited, w_core.at[0], {"ctx": sibling}).wait_recv()
+                for condition, copy in sends:
+                    when(condition, lambda copy=copy: copy().start())
+
+            when(here, act)
+
+    def finish_step(step):
+        for here, _, sends in step:
+
+            def act(sends=sends):
+                for condition, copy in sends:
+                    when(condition, lambda copy=copy: copy().wait_send())
+
+            when(here, act)
+
+    if with_weight:
+        w_all[position, 0] = w_ref[0:1024]
+        w_all[position, 1] = w_ref[1024:2048]
+        run_step(steps[0])
+
+    def prepare(chunk, _):
+        cols = CHUNK_HEADS * HEAD_DIM
+        lanes = pl.ds(pl.multiple_of(chunk * cols, cols), cols)
+        for which, ref in enumerate((k_ref, v_ref)):
+            rows = ref[:, lanes]
+            first = pool(rows)
+            second = pool(first)
+            eighth = pool(second)
+            sixteenth = pool(eighth)
+            for at in range(CHUNK_HEADS):
+                head = chunk * CHUNK_HEADS + at
+                cut = slice(at * HEAD_DIM, (at + 1) * HEAD_DIM)
+                to_right[head, which, 0:128] = rows[384:512, cut]
+                to_right[head, which, 128:192] = first[128:192, cut]
+                to_right[head, which, 192:256] = second[0:64, cut]
+                to_left[head, which, 0:128] = rows[0:128, cut]
+                to_left[head, which, 128:192] = first[64:128, cut]
+                to_left[head, which, 192:256] = second[64:128, cut]
+                third[head, which] = eighth[:, cut]
+                fourth[head, which] = sixteenth[:, cut]
+        for which, taker in enumerate(takers):
+            when(inside(taker), lambda which=which: slot_copy(chunk, which).start())
+        return 0
+
+    lax.fori_loop(0, CHUNKS, prepare, 0)
+    if with_weight:
+        run_step(steps[1])
+
+    def one_head(head, _):
+        chunk = head // CHUNK_HEADS
+
+        @pl.when(head % CHUNK_HEADS == 0)
+        def _():
+            for which, giver in enumerate(givers):
+                when(inside(giver), lambda which=which: slot_copy(chunk, which).wait_recv())
+
+        if with_weight:
+            for at, step in enumerate(steps[2:]):
+                pl.when(head == 1 + 2 * at)(functools.partial(run_step, step))
+        lanes = pl.ds(pl.multiple_of(head * HEAD_DIM, HEAD_DIM), HEAD_DIM)
+        pair = lambda ref: jnp.concatenate([ref[head, 0], ref[head, 1]], axis=1)
+        att[:, lanes] = head_attention(
+            position,
+            ctx_size,
+            q_ref[:, lanes],
+            jnp.concatenate([k_ref[:, lanes], v_ref[:, lanes]], axis=1),
+            pair(left),
+            pair(right),
+            [pair(thirds.at[i]) for i in range(3)],
+            [pair(fourths.at[i]) for i in range(6)],
+            scratch,
+        )
+        return 0
+
+    lax.fori_loop(0, HEADS, one_head, 0)
+
+    if with_weight:
+        for level in range(depth):
+            for other in (0, 2):
+                for half in range(2):
+                    shard = 4 * level + other + 1 - position % 2
+                    piece(shard, half, w_core.at[0], {"ctx": sibling}).wait_recv()
+
+        def project(at, _):
+            count = 2048
+            weight = jnp.concatenate(
+                [w_all[2 * at].reshape(count, 128), w_all[2 * at + 1].reshape(count, 128)], axis=1
+            )
+            result = jnp.dot(att[...], weight, preferred_element_type=F32)
+            out_ref[:, pl.ds(pl.multiple_of(at * 256, 256), 256)] = result.astype(BF16)
+            return 0
+
+        lax.fori_loop(0, ctx_size // 2, project, 0)
+        for step in steps:
+            finish_step(step)
+    else:
+        out_ref[...] = att[...]
+
+    def settle(chunk, _):
+        for which, taker in enumerate(takers):
+            when(inside(taker), lambda which=which: slot_copy(chunk, which).wait_send())
+        return 0
+
+    lax.fori_loop(0, CHUNKS, settle, 0)
+
+
+def layer(ctx_size, queries, keys, values, weight=None):
     rows, width = queries.shape
-    own = pl.BlockSpec((rows, HEAD_DIM), lambda h: (0, h))
-    beside = lambda n: pl.BlockSpec((2, n, HEAD_DIM), lambda h: (0, 0, h))
+    per_head = lambda *lead: pltpu.VMEM((*lead, HEAD_DIM), BF16)
+    slots = len(SLOT_OFFSETS)
+    scratch = [
+        per_head(HEADS, 2, 256),
+        per_head(HEADS, 2, 256),
+        per_head(HEADS, 2, 64),
+        per_head(HEADS, 2, 32),
+        per_head(HEADS, 2, 256),
+        per_head(HEADS, 2, 256),
+        per_head(3, HEADS, 2, 64),
+        per_head(6, HEADS, 2, 32),
+        pltpu.VMEM((3, rows, HEAD_DIM), F32),
+        pltpu.VMEM((rows, width), BF16),
+        pltpu.SemaphoreType.DMA((CHUNKS, slots)),
+        pltpu.SemaphoreType.DMA((CHUNKS, slots)),
+    ]
+    operands = [queries, keys, values]
+    if weight is not None:
+        operands.append(weight)
+        scratch += [
+            pltpu.VMEM((ctx_size, 2, weight.shape[0] // 2, weight.shape[1]), BF16),
+            pltpu.SemaphoreType.DMA((ctx_size, 2)),
+            pltpu.SemaphoreType.DMA((5, ctx_size)),
+            pltpu.SemaphoreType.DMA((ctx_size,)),
+        ]
     return pl.pallas_call(
-        functools.partial(attention_kernel, ctx_size),
-        grid=(HEADS,),
-        in_specs=[pl.BlockSpec(memory_space=pltpu.SMEM), own, own, own, beside(256), beside(256)]
-        + [beside(64)] * 3
-        + [beside(32)] * 6,
-        out_specs=own,
+        functools.partial(layer_kernel, ctx_size, weight is not None),
+        in_specs=[pl.BlockSpec(memory_space=pltpu.VMEM)] * len(operands),
+        out_specs=pl.BlockSpec(memory_space=pltpu.VMEM),
         out_shape=jax.ShapeDtypeStruct((rows, width), BF16),
-        scratch_shapes=[pltpu.VMEM((3, rows, HEAD_DIM), F32)],
-        compiler_params=pltpu.CompilerParams(vmem_limit_bytes=40 << 20),
-        name="attention",
-    )(position[None].astype(jnp.int32), queries, keys, values, left, right, *thirds, *fourths)
-
-
-def project_kernel(x_ref, w_ref, out_ref):
-    weight = jnp.concatenate([w_ref[0], w_ref[1]], axis=1)
-    out_ref[...] = jnp.dot(x_ref[...], weight, preferred_element_type=F32).astype(BF16)
-
-
-def project(attended, shards):
-    rows, width = attended.shape
-    count, _, cols = shards.shape
-    return pl.pallas_call(
-        project_kernel,
-        grid=(count // 2,),
-        in_specs=[
-            pl.BlockSpec((rows, width), lambda j: (0, 0)),
-            pl.BlockSpec((2, width, cols), lambda j: (j, 0, 0)),
-        ],
-        out_specs=pl.BlockSpec((rows, 2 * cols), lambda j: (0, j)),
-        out_shape=jax.ShapeDtypeStruct((rows, count * cols), BF16),
-        compiler_params=pltpu.CompilerParams(vmem_limit_bytes=40 << 20),
-        name="project",
-    )(attended, shards)
-
-
-def moved(array, ctx_size, offset_of):
-    route = []
-    for target in range(ctx_size):
-        source = target + offset_of(target)
-        if 0 <= source < ctx_size:
-            route.append((source, target))
-    return lax.ppermute(array, "ctx", route)
-
-
-THIRD_OFFSETS = [lambda i: -2, lambda i: 2, lambda i: (3, -3)[i % 2]]
-FOURTH_OFFSETS = [
-    lambda i: -4,
-    lambda i: 4,
-    lambda i: (-3, 3, -3, 3)[i % 4],
-    lambda i: (5, -5, 5, -5)[i % 4],
-    lambda i: (6, 6, -6, -6)[i % 4],
-    lambda i: (7, 5, -5, -7)[i % 4],
-]
+        scratch_shapes=scratch,
+        compiler_params=pltpu.CompilerParams(
+            collective_id=0, has_side_effects=True, vmem_limit_bytes=56 << 20
+        ),
+        name="layer",
+    )(*operands)
 
 
 def per_device(query_vectors, key_vectors, value_vectors, out_weight):
     ctx_size = lax.axis_size("ctx")
-    position = lax.axis_index("ctx")
-    whole_shards = out_weight.shape[1] % 128 == 0
-    if whole_shards:
-        weight = lax.all_gather(out_weight, "ctx", axis=0)
-    else:
-        weight = lax.all_gather(out_weight, "ctx", axis=1, tiled=True)
-    to_right, to_left, third, fourth = make_messages(key_vectors, value_vectors)
-    left = moved(to_right, ctx_size, lambda i: -1)
-    right = moved(to_left, ctx_size, lambda i: 1)
-    thirds = [moved(third, ctx_size, offset) for offset in THIRD_OFFSETS]
-    fourths = [moved(fourth, ctx_size, offset) for offset in FOURTH_OFFSETS]
-    attended = attention(
-        ctx_size, position, query_vectors, key_vectors, value_vectors, left, right, thirds, fourths
-    )
-    if whole_shards:
-        return project(attended, weight)
+    in_kernel = (
+        out_weight.shape[1] == 128 and ctx_size % 4 == 0 and lax.axis_size("groups") == 2
+    )
+    if in_kernel:
+        return layer(ctx_size, query_vectors, key_vectors, value_vectors, out_weight)
+    weight = lax.all_gather(out_weight, "ctx", axis=1, tiled=True)
+    attended = layer(ctx_size, query_vectors, key_vectors, value_vectors)
     return jnp.dot(attended, weight, preferred_element_type=F32).astype(BF16)
 
 

time: 227 us -> 154 us (0.68)
  the two profiles are of different devices: /device:TPU:8 before, /device:TPU:0 now
where the time goes in v2:
time: 154 us
  Pallas kernels  151 us (98%)
  local copies, waits for them, and re-layouts  3.16 us (2%)
    pallas_call x1, Pallas kernels, layer(): pl.pallas_call(functools.partial(layer_kernel, ctx_size, weight is not No...  151 us
    unnamed x1, local copies, waits for them, and re-layouts  3.16 us

profile of v2, /device:TPU:0, one launch (start us, length us, event | category | flops | bytes accessed | tf_op | source)
XLA Modules:
  0.0 154.0 jit_solution(10934792377425490439)
XLA Ops:
  0.0 150.9 %layer.1 = bf16[512,2048]{1,0:T(8,128)(2,1)} custom-call(bf16[512,2048]{1,0:T(8,128)(2,1)} %refs_0_.1, bf16[512,2048]{1,0:T(8,128)(2,1)} %refs_1_.1, bf16[512,2048]{1,0:T(8,128)(2,1)} %refs_2_.1, bf16[2048,128]{1,0:T(8,128)(2,1)} %refs_3_.1), custom_call_target="tpu_custom_call" | custom-call | tf_op jit(solution)/shard_map/layer/pallas_call | solution.py:462
  150.9 3.2 %copy.6 = bf16[512,2048]{1,0:T(8,128)(2,1)} copy(bf16[512,2048]{1,0:T(8,128)(2,1)} %layer.1) | data formatting | bytes 4194304

commit v3 on v2

--- a/solution.py
+++ b/solution.py
@@ -108,28 +108,21 @@
         ]
 
     has_left, has_right = edge_flags(4, position, ctx_size)
-    turn = position % 4
-    tests = [has_left, has_right]
-    from_right = [
-        (turn == 1) | (turn == 3),
-        (turn == 0) | (turn == 2),
-        (turn == 0) | (turn == 1),
-        (turn == 0) | (turn == 1),
-    ]
-    pieces = [(fourths[0], has_left), (fourths[1], has_right)]
-    for chunk, is_right in zip(fourths[2:], from_right):
-        pieces.append((chunk, (is_right & has_right) | (~is_right & has_left)))
+    is_right = position % 4 < 2
+    mixed = (is_right & has_right) | (~is_right & has_left)
+    pieces = []
+    for chunks in (fourths[:3], fourths[3:]):
+        pieces += list(zip(chunks, (has_left, has_right, mixed)))
     peak, total, weight = window(q_at[4], pieces)
     state = (peak, total * 16.0, weight * 16.0)
 
     has_left, has_right = edge_flags(3, position, ctx_size)
-    is_right = position % 2 == 0
-    mixed = (is_right & has_right) | (~is_right & has_left)
+    odd = position % 2 == 1
+    own = (odd & has_right) | (~odd & has_left)
+    other = (odd & has_left) | (~odd & has_right)
     state = merged(
         3,
-        window(
-            q_at[3], [(thirds[0], has_left), (thirds[1], has_right), (thirds[2], mixed)]
-        ),
+        window(q_at[3], [(thirds[0], own), (thirds[1], other), (thirds[2], other)]),
         state,
         scratch,
     )
@@ -160,16 +153,12 @@
 SLOT_OFFSETS = [
     (-1, -1, -1, -1),
     (1, 1, 1, 1),
-    (-2, -2, -2, -2),
-    (2, 2, 2, 2),
-    (3, -3, 3, -3),
+    (-2, 2, -2, 2),
     (-4, -4, -4, -4),
     (4, 4, 4, 4),
-    (-3, 3, -3, 3),
-    (5, -5, 5, -5),
     (6, 6, -6, -6),
-    (7, 5, -5, -7),
 ]
+PASSED = 5
 REACH = 7
 CHUNKS = 8
 CHUNK_HEADS = HEADS // CHUNKS
@@ -197,8 +186,9 @@
     else:
         q_ref, k_ref, v_ref, out_ref = refs[:4]
         refs = refs[4:]
-    (to_right, to_left, third, fourth, left, right, thirds, fourths,
-     scratch, att, send_sem, recv_sem) = refs[:12]
+    (to_right, to_left, third, fourth, rims, thirds, fourths, pooled, their_thirds,
+     their_pooled, their_fourths, scratch, att, send_sem, recv_sem, pass_send,
+     pass_recv) = refs[:17]
 
     position = lax.axis_index("ctx")
     group = lax.axis_index("groups")
@@ -223,19 +213,33 @@
         )
         peers = peers + 1
 
-    slots = [left, right] + [thirds.at[i] for i in range(3)] + [fourths.at[i] for i in range(6)]
-    sources = [to_right, to_left] + [third] * 3 + [fourth] * 6
+    slots = [rims.at[0], rims.at[1], thirds] + [fourths.at[i] for i in range(3)]
+    sources = [to_right, to_left, third] + [fourth] * 3
+    passed = [thirds, pooled] + [fourths.at[i] for i in range(3)]
+    passed_to = [their_thirds, their_pooled] + [their_fourths.at[i] for i in range(3)]
+    sibling = position + 1 - 2 * (position % 2)
     givers = [position + by_turn(turn, table) for table in SLOT_OFFSETS]
     takers = [position + by_turn(turn, inverse(table)) for table in SLOT_OFFSETS]
     inside = lambda peer: (peer >= 0) & (peer < ctx_size)
 
+    own_there = [inside(giver) for giver in givers]
+    across = inside(position + 2 - 4 * (position % 2))
+    send_there = [own_there[2], own_there[2]] + own_there[3:]
+    pass_there = [across, across] + own_there[3:]
+
     pl.semaphore_wait(barrier, peers)
 
-    for slot, giver in zip(slots, givers):
-
-        @pl.when(jnp.logical_not(inside(giver)))
+    for slot, there in zip(slots + passed_to, own_there + pass_there):
+
+        @pl.when(jnp.logical_not(there))
         def _():
             slot[...] = jnp.zeros(slot.shape, BF16)
+
+    def when(condition, action):
+        if condition is None:
+            action()
+        else:
+            pl.when(condition)(action)
 
     def slot_copy(chunk, which):
         heads = pl.ds(chunk * CHUNK_HEADS, CHUNK_HEADS)
@@ -248,12 +252,40 @@
             device_id_type=pl.DeviceIdType.MESH,
         )
 
+    def pass_copy(chunk, which):
+        heads = pl.ds(chunk * CHUNK_HEADS, CHUNK_HEADS)
+        return pltpu.make_async_remote_copy(
+            src_ref=passed[which].at[heads],
+            dst_ref=passed_to[which].at[heads],
+            send_sem=pass_send.at[chunk, which],
+            recv_sem=pass_recv.at[chunk, which],
+            device_id={"ctx": sibling},
+            device_id_type=pl.DeviceIdType.MESH,
+        )
+
+    def forward(chunk):
+        for which, there in enumerate(own_there):
+            when(there, lambda which=which: slot_copy(chunk, which).wait_recv())
+        lanes = []
+        for at in range(CHUNK_HEADS):
+            for which in range(2):
+                lanes.append(rims[position % 2, chunk * CHUNK_HEADS + at, which])
+        rows = jnp.concatenate(lanes, axis=1)
+        eighth = jnp.concatenate(
+            [pool(rows[192:256]), pool(pool(rows[128:192])), pool(pool(pool(rows[0:128])))], axis=0
+        )
+        for at in range(CHUNK_HEADS):
+            for which in range(2):
+                start = (2 * at + which) * HEAD_DIM
+                pooled[chunk * CHUNK_HEADS + at, which] = eighth[:, start : start + HEAD_DIM]
+        for which, there in enumerate(send_there):
+            when(there, lambda which=which: pass_copy(chunk, which).start())
+
     steps = []
     if with_weight:
         z = position // 4
         depth = ctx_size // 4
         partner = position + 2 - 4 * ((position // 2) % 2)
-        sibling = position + 1 - 2 * (position % 2)
 
         def piece(shard, half, send, device):
             return pltpu.make_async_remote_copy(
@@ -315,12 +347,6 @@
                 step.append((always, (shard, 1 - group), sends))
         steps.append(step)
 
-    def when(condition, action):
-        if condition is None:
-            action()
-        else:
-            pl.when(condition)(action)
-
     def run_step(step):
         for here, awaited, sends in step:
 
@@ -377,10 +403,18 @@
     def one_head(head, _):
         chunk = head // CHUNK_HEADS
 
+        @pl.when(head == 0)
+        def _():
+            forward(0)
+
+        @pl.when((head % CHUNK_HEADS == CHUNK_HEADS - 1) & (chunk + 1 < CHUNKS))
+        def _():
+            forward(chunk + 1)
+
         @pl.when(head % CHUNK_HEADS == 0)
         def _():
-            for which, giver in enumerate(givers):
-                when(inside(giver), lambda which=which: slot_copy(chunk, which).wait_recv())
+            for which, there in enumerate(pass_there):
+                when(there, lambda which=which: pass_copy(chunk, which).wait_recv())
 
         if with_weight:
             for at, step in enumerate(steps[2:]):
@@ -392,10 +426,10 @@
             ctx_size,
             q_ref[:, lanes],
             jnp.concatenate([k_ref[:, lanes], v_ref[:, lanes]], axis=1),
-            pair(left),
-            pair(right),
-            [pair(thirds.at[i]) for i in range(3)],
-            [pair(fourths.at[i]) for i in range(6)],
+            pair(rims.at[0]),
+            pair(rims.at[1]),
+            [pair(ref) for ref in (thirds, their_thirds, their_pooled)],
+            [pair(ref.at[i]) for ref in (fourths, their_fourths) for i in range(3)],
             scratch,
         )
         return 0
@@ -427,6 +461,8 @@
     def settle(chunk, _):
         for which, taker in enumerate(takers):
             when(inside(taker), lambda which=which: slot_copy(chunk, which).wait_send())
+        for which, there in enumerate(send_there):
+            when(there, lambda which=which: pass_copy(chunk, which).wait_send())
         return 0
 
     lax.fori_loop(0, CHUNKS, settle, 0)
@@ -441,14 +477,19 @@
         per_head(HEADS, 2, 256),
         per_head(HEADS, 2, 64),
         per_head(HEADS, 2, 32),
-        per_head(HEADS, 2, 256),
-        per_head(HEADS, 2, 256),
-        per_head(3, HEADS, 2, 64),
-        per_head(6, HEADS, 2, 32),
+        per_head(2, HEADS, 2, 256),
+        per_head(HEADS, 2, 64),
+        per_head(3, HEADS, 2, 32),
+        per_head(HEADS, 2, 64),
+        per_head(HEADS, 2, 64),
+        per_head(HEADS, 2, 64),
+        per_head(3, HEADS, 2, 32),
         pltpu.VMEM((3, rows, HEAD_DIM), F32),
         pltpu.VMEM((rows, width), BF16),
         pltpu.SemaphoreType.DMA((CHUNKS, slots)),
         pltpu.SemaphoreType.DMA((CHUNKS, slots)),
+        pltpu.SemaphoreType.DMA((CHUNKS, PASSED)),
+        pltpu.SemaphoreType.DMA((CHUNKS, PASSED)),
     ]
     operands = [queries, keys, values]
     if weight is not None:

time: 154 us -> 137 us (0.89)
  the two profiles are of different devices: /device:TPU:0 before, /device:TPU:1 now
where the time goes in v3:
time: 137 us; the launch traced here: 135 us
  Pallas kernels  132 us (96%)
  local copies, waits for them, and re-layouts  3.16 us (2%)
    pallas_call x1, Pallas kernels, layer(): pl.pallas_call(functools.partial(layer_kernel, ctx_size, weight is not No...  132 us
    unnamed x1, local copies, waits for them, and re-layouts  3.16 us

profile of v3, /device:TPU:1, one launch (start us, length us, event | category | flops | bytes accessed | tf_op | source)
XLA Modules:
  0.0 134.8 jit_solution(4149093089729589382)
XLA Ops:
  0.0 131.7 %layer.1 = bf16[512,2048]{1,0:T(8,128)(2,1)} custom-call(bf16[512,2048]{1,0:T(8,128)(2,1)} %refs_0_.1, bf16[512,2048]{1,0:T(8,128)(2,1)} %refs_1_.1, bf16[512,2048]{1,0:T(8,128)(2,1)} %refs_2_.1, bf16[2048,128]{1,0:T(8,128)(2,1)} %refs_3_.1), custom_call_target="tpu_custom_call" | custom-call | tf_op jit(solution)/shard_map/layer/pallas_call | solution.py:503
  131.7 3.2 %copy.6 = bf16[512,2048]{1,0:T(8,128)(2,1)} copy(bf16[512,2048]{1,0:T(8,128)(2,1)} %layer.1) | data formatting | bytes 4194304

commit v4 on v3

--- a/solution.py
+++ b/solution.py
@@ -18,27 +18,48 @@
 MASKED = -1e30
 
 
-def pool(rows):
-    count = rows.shape[0] // 2
-    at = lax.broadcasted_iota(jnp.int32, (count, 2 * count), 0)
-    source = lax.broadcasted_iota(jnp.int32, (count, 2 * count), 1)
-    half = jnp.where((source >> 1) == at, 0.5, 0.0).astype(BF16)
-    return jnp.dot(half, rows, preferred_element_type=F32).astype(BF16)
-
-
-def attend(queries, keys, values, bias=None):
+def pooling_matrix():
+    at = lax.broadcasted_iota(jnp.int32, (BLOCK, 2 * BLOCK), 0)
+    source = lax.broadcasted_iota(jnp.int32, (BLOCK, 2 * BLOCK), 1)
+    return jnp.where((source >> 1) == at, 0.5, 0.0).astype(BF16)
+
+
+def pool(rows, halving):
+    means = []
+    for start in range(0, rows.shape[0], 2 * BLOCK):
+        part = rows[start : start + 2 * BLOCK]
+        count = part.shape[0]
+        half = halving[: count // 2, :count]
+        means.append(jnp.dot(half, part, preferred_element_type=F32).astype(BF16))
+    return means[0] if len(means) == 1 else jnp.concatenate(means, axis=0)
+
+
+def raw_scores(queries, keys, _, bias):
     scores = lax.dot_general(queries, keys, (((1,), (1,)), ((), ())), preferred_element_type=F32)
-    if bias is not None:
-        scores = scores + bias
+    return scores if bias is None else scores + bias
+
+
+def softmax_terms(scores, values):
     peak = jnp.max(scores, axis=1, keepdims=True)
     weights = jnp.exp2((scores - peak) * RATE).astype(BF16)
     ones = jnp.ones((values.shape[0], HEAD_DIM), BF16)
     both = jnp.dot(weights, jnp.concatenate([values, ones], axis=1), preferred_element_type=F32)
     return (
-        jnp.broadcast_to(peak, (queries.shape[0], HEAD_DIM)),
+        jnp.broadcast_to(peak, (scores.shape[0], HEAD_DIM)),
         both[:, :HEAD_DIM],
         both[:, HEAD_DIM:],
     )
+
+
+def attend_all(windows):
+    ahead = 3
+    scores, terms = {}, []
+    for at in range(len(windows) + ahead):
+        if at < len(windows):
+            scores[at] = raw_scores(*windows[at])
+        if at >= ahead:
+            terms.append(softmax_terms(scores.pop(at - ahead), windows[at - ahead][2]))
+    return terms
 
 
 def stack(parts):
@@ -77,29 +98,26 @@
     return block >= 1, block + 1 < ctx_size // span
 
 
-def head_attention(position, ctx_size, q, kv, left, right, thirds, fourths, scratch):
-    k_of = lambda x: x[:, :HEAD_DIM]
-    v_of = lambda x: x[:, HEAD_DIM:]
+def head_windows(position, ctx_size, halving, q, kv, left, right, thirds, fourths):
     everything = jnp.concatenate([kv, q], axis=1)
     levels = [everything]
     for _ in range(4):
-        levels.append(pool(levels[-1]))
+        levels.append(pool(levels[-1], halving))
     q_at = [level[:, 2 * HEAD_DIM :] for level in levels]
     kv_at = [level[:, : 2 * HEAD_DIM] for level in levels]
 
-    left0, left1b = left[0:128], left[128:192]
-    right0, right1b = right[0:128], right[128:192]
-    left1 = jnp.concatenate([left1b, pool(left0)], axis=0)
-    right1 = jnp.concatenate([pool(right0), right1b], axis=0)
-    left2 = jnp.concatenate([left[192:256], pool(left1)], axis=0)
-    right2 = jnp.concatenate([pool(right1), right[192:256]], axis=0)
+    left0, right0 = left[0:128], right[0:128]
+    left1 = jnp.concatenate([left[128:192], pool(left0, halving)], axis=0)
+    right1 = jnp.concatenate([pool(right0, halving), right[128:192]], axis=0)
+    left2 = jnp.concatenate([left[192:256], pool(left1, halving)], axis=0)
+    right2 = jnp.concatenate([pool(right1, halving), right[192:256]], axis=0)
 
     def window(queries, pieces):
         rows = jnp.concatenate([piece for piece, _ in pieces], axis=0)
         bias = None
         if any(allowed is not None for _, allowed in pieces):
             bias = bias_row([(piece.shape[0], allowed) for piece, allowed in pieces])
-        return attend(queries, k_of(rows), v_of(rows), bias)
+        return queries, rows[:, :HEAD_DIM], rows[:, HEAD_DIM:], bias
 
     def halves(queries, before, has_before, after, has_after):
         return [
@@ -113,41 +131,35 @@
     pieces = []
     for chunks in (fourths[:3], fourths[3:]):
         pieces += list(zip(chunks, (has_left, has_right, mixed)))
-    peak, total, weight = window(q_at[4], pieces)
-    state = (peak, total * 16.0, weight * 16.0)
+    windows = [window(q_at[4], pieces)]
 
     has_left, has_right = edge_flags(3, position, ctx_size)
     odd = position % 2 == 1
     own = (odd & has_right) | (~odd & has_left)
     other = (odd & has_left) | (~odd & has_right)
-    state = merged(
-        3,
-        window(q_at[3], [(thirds[0], own), (thirds[1], other), (thirds[2], other)]),
-        state,
-        scratch,
-    )
+    windows.append(window(q_at[3], [(thirds[0], own), (thirds[1], other), (thirds[2], other)]))
 
     has_left, has_right = edge_flags(2, position, ctx_size)
-    state = merged(2, stack(halves(q_at[2], left2, has_left, right2, has_right)), state, scratch)
+    windows += halves(q_at[2], left2, has_left, right2, has_right)
 
     kv1 = kv_at[1]
-    state = merged(
-        1,
-        stack(
-            halves(q_at[1][:128], left1, has_left, kv1[128:], None)
-            + halves(q_at[1][128:], kv1[:128], None, right1, has_right)
-        ),
-        state,
-        scratch,
-    )
-
-    parts = [window(q[0:128], [(left0, has_left), (kv[0:256], None)])]
+    windows += halves(q_at[1][:128], left1, has_left, kv1[128:], None)
+    windows += halves(q_at[1][128:], kv1[:128], None, right1, has_right)
+
+    windows.append(window(q[0:128], [(left0, has_left), (kv[0:256], None)]))
     for block in (1, 2):
         start = 128 * block
-        parts.append(window(q[start : start + 128], [(kv[start - 128 : start + 256], None)]))
-    parts.append(window(q[384:512], [(kv[256:512], None), (right0, has_right)]))
-    _, total, weight = merged(0, stack(parts), state, scratch)
-    return (total / weight).astype(BF16)
+        windows.append(window(q[start : start + 128], [(kv[start - 128 : start + 256], None)]))
+    windows.append(window(q[384:512], [(kv[256:512], None), (right0, has_right)]))
+    return windows
+
+
+def merge_windows(terms, scratch):
+    peak, total, weight = terms[0]
+    state = (peak, total * 16.0, weight * 16.0)
+    for height, cut in ((3, slice(1, 2)), (2, slice(2, 4)), (1, slice(4, 8)), (0, slice(8, 12))):
+        state = merged(height, stack(terms[cut]), state, scratch)
+    return (state[1] / state[2]).astype(BF16)
 
 
 SLOT_OFFSETS = [
@@ -161,6 +173,7 @@
 PASSED = 5
 REACH = 7
 CHUNKS = 8
+AHEAD = 3
 CHUNK_HEADS = HEADS // CHUNKS
 
 
@@ -187,9 +200,10 @@
         q_ref, k_ref, v_ref, out_ref = refs[:4]
         refs = refs[4:]
     (to_right, to_left, third, fourth, rims, thirds, fourths, pooled, their_thirds,
-     their_pooled, their_fourths, scratch, att, send_sem, recv_sem, pass_send,
-     pass_recv) = refs[:17]
-
+     their_pooled, their_fourths, scratch, att, halving, send_sem, recv_sem,
+     pass_send, pass_recv) = refs[:18]
+
+    halving[...] = pooling_matrix()
     position = lax.axis_index("ctx")
     group = lax.axis_index("groups")
     turn = position % 4
@@ -272,7 +286,12 @@
                 lanes.append(rims[position % 2, chunk * CHUNK_HEADS + at, which])
         rows = jnp.concatenate(lanes, axis=1)
         eighth = jnp.concatenate(
-            [pool(rows[192:256]), pool(pool(rows[128:192])), pool(pool(pool(rows[0:128])))], axis=0
+            [
+                pool(rows[192:256], halving),
+                pool(pool(rows[128:192], halving), halving),
+                pool(pool(pool(rows[0:128], halving), halving), halving),
+            ],
+            axis=0,
         )
         for at in range(CHUNK_HEADS):
             for which in range(2):
@@ -377,10 +396,10 @@
         lanes = pl.ds(pl.multiple_of(chunk * cols, cols), cols)
         for which, ref in enumerate((k_ref, v_ref)):
             rows = ref[:, lanes]
-            first = pool(rows)
-            second = pool(first)
-            eighth = pool(second)
-            sixteenth = pool(eighth)
+            first = pool(rows, halving)
+            second = pool(first, halving)
+            eighth = pool(second, halving)
+            sixteenth = pool(eighth, halving)
             for at in range(CHUNK_HEADS):
                 head = chunk * CHUNK_HEADS + at
                 cut = slice(at * HEAD_DIM, (at + 1) * HEAD_DIM)
@@ -396,45 +415,53 @@
             when(inside(taker), lambda which=which: slot_copy(chunk, which).start())
         return 0
 
-    lax.fori_loop(0, CHUNKS, prepare, 0)
+    lax.fori_loop(0, AHEAD, prepare, 0)
     if with_weight:
         run_step(steps[1])
-
-    def one_head(head, _):
-        chunk = head // CHUNK_HEADS
-
-        @pl.when(head == 0)
+    forward(0)
+
+    def one_chunk(chunk, _):
+        @pl.when(chunk + AHEAD < CHUNKS)
         def _():
-            forward(0)
-
-        @pl.when((head % CHUNK_HEADS == CHUNK_HEADS - 1) & (chunk + 1 < CHUNKS))
+            prepare(chunk + AHEAD, 0)
+
+        @pl.when(chunk + 1 < CHUNKS)
         def _():
             forward(chunk + 1)
 
-        @pl.when(head % CHUNK_HEADS == 0)
-        def _():
-            for which, there in enumerate(pass_there):
-                when(there, lambda which=which: pass_copy(chunk, which).wait_recv())
+        for which, there in enumerate(pass_there):
+            when(there, lambda which=which: pass_copy(chunk, which).wait_recv())
 
         if with_weight:
             for at, step in enumerate(steps[2:]):
-                pl.when(head == 1 + 2 * at)(functools.partial(run_step, step))
-        lanes = pl.ds(pl.multiple_of(head * HEAD_DIM, HEAD_DIM), HEAD_DIM)
-        pair = lambda ref: jnp.concatenate([ref[head, 0], ref[head, 1]], axis=1)
-        att[:, lanes] = head_attention(
-            position,
-            ctx_size,
-            q_ref[:, lanes],
-            jnp.concatenate([k_ref[:, lanes], v_ref[:, lanes]], axis=1),
-            pair(rims.at[0]),
-            pair(rims.at[1]),
-            [pair(ref) for ref in (thirds, their_thirds, their_pooled)],
-            [pair(ref.at[i]) for ref in (fourths, their_fourths) for i in range(3)],
-            scratch,
-        )
+                pl.when(chunk == (1, 2, 4, 6)[at])(functools.partial(run_step, step))
+        windows = []
+        for at in range(CHUNK_HEADS):
+            head = chunk * CHUNK_HEADS + at
+            lanes = pl.ds(pl.multiple_of(head * HEAD_DIM, HEAD_DIM), HEAD_DIM)
+            pair = lambda ref: jnp.concatenate([ref[head, 0], ref[head, 1]], axis=1)
+            windows.append(
+                head_windows(
+                    position,
+                    ctx_size,
+                    halving,
+                    q_ref[:, lanes],
+                    jnp.concatenate([k_ref[:, lanes], v_ref[:, lanes]], axis=1),
+                    pair(rims.at[0]),
+                    pair(rims.at[1]),
+                    [pair(ref) for ref in (thirds, their_thirds, their_pooled)],
+                    [pair(ref.at[i]) for ref in (fourths, their_fourths) for i in range(3)],
+                )
+            )
+        count = len(windows[0])
+        terms = attend_all([one[at] for at in range(count) for one in windows])
+        for at in range(CHUNK_HEADS):
+            head = chunk * CHUNK_HEADS + at
+            lanes = pl.ds(pl.multiple_of(head * HEAD_DIM, HEAD_DIM), HEAD_DIM)
+            att[:, lanes] = merge_windows(terms[at::CHUNK_HEADS], scratch.at[at])
         return 0
 
-    lax.fori_loop(0, HEADS, one_head, 0)
+    lax.fori_loop(0, CHUNKS, one_chunk, 0)
 
     if with_weight:
         for level in range(depth):
@@ -484,8 +511,9 @@
         per_head(HEADS, 2, 64),
         per_head(HEADS, 2, 64),
         per_head(3, HEADS, 2, 32),
-        pltpu.VMEM((3, rows, HEAD_DIM), F32),
+        pltpu.VMEM((CHUNK_HEADS, 3, rows, HEAD_DIM), F32),
         pltpu.VMEM((rows, width), BF16),
+        pltpu.VMEM((BLOCK, 2 * BLOCK), BF16),
         pltpu.SemaphoreType.DMA((CHUNKS, slots)),
         pltpu.SemaphoreType.DMA((CHUNKS, slots)),
         pltpu.SemaphoreType.DMA((CHUNKS, PASSED)),

time: 137 us -> 105 us (0.77)
  the two profiles are of different devices: /device:TPU:1 before, /device:TPU:26 now
where the time goes in v4:
time: 105 us
  Pallas kernels  102 us (97%)
  local copies, waits for them, and re-layouts  3.16 us (3%)
    pallas_call x1, Pallas kernels, layer(): pl.pallas_call(functools.partial(layer_kernel, ctx_size, weight is not No...  102 us
    unnamed x1, local copies, waits for them, and re-layouts  3.16 us

profile of v4, /device:TPU:26, one launch (start us, length us, event | category | flops | bytes accessed | tf_op | source)
XLA Modules:
  0.0 105.3 jit_solution(17688640143853829931)
XLA Ops:
  0.0 102.2 %layer.1 = bf16[512,2048]{1,0:T(8,128)(2,1)} custom-call(bf16[512,2048]{1,0:T(8,128)(2,1)} %refs_0_.1, bf16[512,2048]{1,0:T(8,128)(2,1)} %refs_1_.1, bf16[512,2048]{1,0:T(8,128)(2,1)} %refs_2_.1, bf16[2048,128]{1,0:T(8,128)(2,1)} %refs_3_.1), custom_call_target="tpu_custom_call" | custom-call | tf_op jit(solution)/shard_map/layer/pallas_call | solution.py:531
  102.2 3.2 %copy.6 = bf16[512,2048]{1,0:T(8,128)(2,1)} copy(bf16[512,2048]{1,0:T(8,128)(2,1)} %layer.1) | data formatting | bytes 4194304

commit v5 on v4

--- a/solution.py
+++ b/solution.py
@@ -173,7 +173,8 @@
 PASSED = 5
 REACH = 7
 CHUNKS = 8
-AHEAD = 3
+AHEAD = 4
+WEIGHT_CHUNKS = (0, 2, 4, 3, 3, 5, 7)
 CHUNK_HEADS = HEADS // CHUNKS
 
 
@@ -355,16 +356,17 @@
                     ]
                     step.append((here, (shard, group), sends))
             steps.append(step)
-        step = []
-        for turns in range(depth):
-            for base in (position, partner):
-                if turns == 0 and base is position:
-                    continue
-                level = lax.rem(z + turns, depth)
-                shard = base + 4 * (level - z)
-                sends = [(always, functools.partial(to_core, shard, 1 - group, False))]
-                step.append((always, (shard, 1 - group), sends))
-        steps.append(step)
+        for hops in range(depth):
+            step = []
+            for way in (1, -1):
+                here = (z - hops * way >= 0) & (z - hops * way < depth)
+                for base in (position, partner):
+                    if hops == 0 and (way < 0 or base is position):
+                        continue
+                    shard = base - 4 * hops * way
+                    sends = [(always, functools.partial(to_core, shard, 1 - group, False))]
+                    step.append((here, (shard, 1 - group), sends))
+            steps.append(step)
 
     def run_step(step):
         for here, awaited, sends in step:
@@ -434,7 +436,7 @@
 
         if with_weight:
             for at, step in enumerate(steps[2:]):
-                pl.when(chunk == (1, 2, 4, 6)[at])(functools.partial(run_step, step))
+                pl.when(chunk == WEIGHT_CHUNKS[at])(functools.partial(run_step, step))
         windows = []
         for at in range(CHUNK_HEADS):
             head = chunk * CHUNK_HEADS + at
@@ -464,13 +466,10 @@
     lax.fori_loop(0, CHUNKS, one_chunk, 0)
 
     if with_weight:
-        for level in range(depth):
-            for other in (0, 2):
-                for half in range(2):
-                    shard = 4 * level + other + 1 - position % 2
-                    piece(shard, half, w_core.at[0], {"ctx": sibling}).wait_recv()
-
         def project(at, _):
+            for half in range(2):
+                theirs = 2 * at + 1 - position % 2
+                piece(theirs, half, w_core.at[0], {"ctx": sibling}).wait_recv()
             count = 2048
             weight = jnp.concatenate(
                 [w_all[2 * at].reshape(count, 128), w_all[2 * at + 1].reshape(count, 128)], axis=1
@@ -544,7 +543,7 @@
 def per_device(query_vectors, key_vectors, value_vectors, out_weight):
     ctx_size = lax.axis_size("ctx")
     in_kernel = (
-        out_weight.shape[1] == 128 and ctx_size % 4 == 0 and lax.axis_size("groups") == 2
+        out_weight.shape[1] == 128 and ctx_size == 16 and lax.axis_size("groups") == 2
     )
     if in_kernel:
         return layer(ctx_size, query_vectors, key_vectors, value_vectors, out_weight)

time: 105 us -> 106 us (level)
  the two profiles are of different devices: /device:TPU:26 before, /device:TPU:1 now
where the time goes in v5:
time: 106 us
  Pallas kernels  103 us (97%)
  local copies, waits for them, and re-layouts  3.16 us (3%)
    pallas_call x1, Pallas kernels, layer(): pl.pallas_call(functools.partial(layer_kernel, ctx_size, weight is not No...  103 us
    unnamed x1, local copies, waits for them, and re-layouts  3.16 us

profile of v5, /device:TPU:1, one launch (start us, length us, event | category | flops | bytes accessed | tf_op | source)
XLA Modules:
  0.0 106.2 jit_solution(2187259560590831620)
XLA Ops:
  0.0 103.0 %layer.1 = bf16[512,2048]{1,0:T(8,128)(2,1)} custom-call(bf16[512,2048]{1,0:T(8,128)(2,1)} %refs_0_.1, bf16[512,2048]{1,0:T(8,128)(2,1)} %refs_1_.1, bf16[512,2048]{1,0:T(8,128)(2,1)} %refs_2_.1, bf16[2048,128]{1,0:T(8,128)(2,1)} %refs_3_.1), custom_call_target="tpu_custom_call" | custom-call | tf_op jit(solution)/shard_map/layer/pallas_call | solution.py:530
  103.0 3.2 %copy.6 = bf16[512,2048]{1,0:T(8,128)(2,1)} copy(bf16[512,2048]{1,0:T(8,128)(2,1)} %layer.1) | data formatting | bytes 4194304

commit v6 on v5

--- a/solution.py
+++ b/solution.py
@@ -34,25 +34,45 @@
     return means[0] if len(means) == 1 else jnp.concatenate(means, axis=0)
 
 
-def raw_scores(queries, keys, _, bias):
+def admission_bias():
+    row = lax.broadcasted_iota(jnp.int32, (BLOCK, 2 * BLOCK), 0)
+    key = lax.broadcasted_iota(jnp.int32, (BLOCK, 2 * BLOCK), 1)
+    upper = row >= HALF
+    left_ok = (key < BLOCK) & (upper | (key < HALF))
+    right_ok = (key >= BLOCK) & (jnp.logical_not(upper) | (key >= BLOCK + HALF))
+    return jnp.where(left_ok | right_ok, 0.0, MASKED)
+
+
+def raw_scores(queries, keys, _, biases):
     scores = lax.dot_general(queries, keys, (((1,), (1,)), ((), ())), preferred_element_type=F32)
-    return scores if bias is None else scores + bias
-
-
-def softmax_terms(scores, values):
-    peak = jnp.max(scores, axis=1, keepdims=True)
-    weights = jnp.exp2((scores - peak) * RATE).astype(BF16)
+    if len(biases) == 1:
+        parts = [scores]
+    else:
+        parts = [scores[:BLOCK, : 3 * BLOCK], scores[BLOCK:, BLOCK:]]
+    return [part if bias is None else part + bias for part, bias in zip(parts, biases)]
+
+
+def softmax_terms(parts, values):
+    peaks, weights = [], []
+    for scores in parts:
+        peak = jnp.max(scores, axis=1, keepdims=True)
+        weights.append(jnp.exp2((scores - peak) * RATE).astype(BF16))
+        peaks.append(jnp.broadcast_to(peak, (scores.shape[0], HEAD_DIM)))
+    if len(parts) == 2:
+        none = jnp.zeros((BLOCK, BLOCK), BF16)
+        weights = [
+            jnp.concatenate([weights[0], none], axis=1),
+            jnp.concatenate([none, weights[1]], axis=1),
+        ]
+    weights = jnp.concatenate(weights, axis=0) if len(weights) == 2 else weights[0]
+    peak = jnp.concatenate(peaks, axis=0) if len(peaks) == 2 else peaks[0]
     ones = jnp.ones((values.shape[0], HEAD_DIM), BF16)
     both = jnp.dot(weights, jnp.concatenate([values, ones], axis=1), preferred_element_type=F32)
-    return (
-        jnp.broadcast_to(peak, (scores.shape[0], HEAD_DIM)),
-        both[:, :HEAD_DIM],
-        both[:, HEAD_DIM:],
-    )
+    return peak, both[:, :HEAD_DIM], both[:, HEAD_DIM:]
 
 
 def attend_all(windows):
-    ahead = 3
+    ahead = 2
     scores, terms = {}, []
     for at in range(len(windows) + ahead):
         if at < len(windows):
@@ -98,7 +118,7 @@
     return block >= 1, block + 1 < ctx_size // span
 
 
-def head_windows(position, ctx_size, halving, q, kv, left, right, thirds, fourths):
+def head_windows(position, ctx_size, halving, admission, q, kv, left, right, thirds, fourths):
     everything = jnp.concatenate([kv, q], axis=1)
     levels = [everything]
     for _ in range(4):
@@ -112,18 +132,16 @@
     left2 = jnp.concatenate([left[192:256], pool(left1, halving)], axis=0)
     right2 = jnp.concatenate([pool(right1, halving), right[192:256]], axis=0)
 
-    def window(queries, pieces):
+    def window(queries, pieces, admitted=None):
         rows = jnp.concatenate([piece for piece, _ in pieces], axis=0)
-        bias = None
+        bias = admitted
         if any(allowed is not None for _, allowed in pieces):
-            bias = bias_row([(piece.shape[0], allowed) for piece, allowed in pieces])
-        return queries, rows[:, :HEAD_DIM], rows[:, HEAD_DIM:], bias
-
-    def halves(queries, before, has_before, after, has_after):
-        return [
-            window(queries[:HALF], [(before[:HALF], has_before), (after, has_after)]),
-            window(queries[HALF:], [(before, has_before), (after[HALF:], has_after)]),
-        ]
+            edge = bias_row([(piece.shape[0], allowed) for piece, allowed in pieces])
+            bias = edge if admitted is None else admitted + edge
+        return queries, rows[:, :HEAD_DIM], rows[:, HEAD_DIM:], (bias,)
+
+    def two_blocks(queries, rows, biases):
+        return queries, rows[:, :HEAD_DIM], rows[:, HEAD_DIM:], biases
 
     has_left, has_right = edge_flags(4, position, ctx_size)
     is_right = position % 4 < 2
@@ -140,24 +158,23 @@
     windows.append(window(q_at[3], [(thirds[0], own), (thirds[1], other), (thirds[2], other)]))
 
     has_left, has_right = edge_flags(2, position, ctx_size)
-    windows += halves(q_at[2], left2, has_left, right2, has_right)
-
-    kv1 = kv_at[1]
-    windows += halves(q_at[1][:128], left1, has_left, kv1[128:], None)
-    windows += halves(q_at[1][128:], kv1[:128], None, right1, has_right)
-
-    windows.append(window(q[0:128], [(left0, has_left), (kv[0:256], None)]))
-    for block in (1, 2):
-        start = 128 * block
-        windows.append(window(q[start : start + 128], [(kv[start - 128 : start + 256], None)]))
-    windows.append(window(q[384:512], [(kv[256:512], None), (right0, has_right)]))
+    windows.append(window(q_at[2], [(left2, has_left), (right2, has_right)], admission))
+
+    q1, kv1 = q_at[1], kv_at[1]
+    windows.append(window(q1[:128], [(left1, has_left), (kv1[128:], None)], admission))
+    windows.append(window(q1[128:], [(kv1[:128], None), (right1, has_right)], admission))
+
+    first = bias_row([(128, has_left), (256, None)])
+    last = bias_row([(256, None), (128, has_right)])
+    windows.append(two_blocks(q[:256], jnp.concatenate([left0, kv[:384]], axis=0), (first, None)))
+    windows.append(two_blocks(q[256:], jnp.concatenate([kv[128:], right0], axis=0), (None, last)))
     return windows
 
 
 def merge_windows(terms, scratch):
     peak, total, weight = terms[0]
     state = (peak, total * 16.0, weight * 16.0)
-    for height, cut in ((3, slice(1, 2)), (2, slice(2, 4)), (1, slice(4, 8)), (0, slice(8, 12))):
+    for height, cut in ((3, slice(1, 2)), (2, slice(2, 3)), (1, slice(3, 5)), (0, slice(5, 7))):
         state = merged(height, stack(terms[cut]), state, scratch)
     return (state[1] / state[2]).astype(BF16)
 
@@ -201,10 +218,11 @@
         q_ref, k_ref, v_ref, out_ref = refs[:4]
         refs = refs[4:]
     (to_right, to_left, third, fourth, rims, thirds, fourths, pooled, their_thirds,
-     their_pooled, their_fourths, scratch, att, halving, send_sem, recv_sem,
-     pass_send, pass_recv) = refs[:18]
+     their_pooled, their_fourths, scratch, att, halving, admission, send_sem,
+     recv_sem, pass_send, pass_recv) = refs[:19]
 
     halving[...] = pooling_matrix()
+    admission[...] = admission_bias()
     position = lax.axis_index("ctx")
     group = lax.axis_index("groups")
     turn = position % 4
@@ -447,6 +465,7 @@
                     position,
                     ctx_size,
                     halving,
+                    admission[...],
                     q_ref[:, lanes],
                     jnp.concatenate([k_ref[:, lanes], v_ref[:, lanes]], axis=1),
                     pair(rims.at[0]),
@@ -513,6 +532,7 @@
         pltpu.VMEM((CHUNK_HEADS, 3, rows, HEAD_DIM), F32),
         pltpu.VMEM((rows, width), BF16),
         pltpu.VMEM((BLOCK, 2 * BLOCK), BF16),
+        pltpu.VMEM((BLOCK, 2 * BLOCK), F32),
         pltpu.SemaphoreType.DMA((CHUNKS, slots)),
         pltpu.SemaphoreType.DMA((CHUNKS, slots)),
         pltpu.SemaphoreType.DMA((CHUNKS, PASSED)),

time: 106 us -> 107 us (level)
  no operation moved by 1% of the time
where the time goes in v6:
time: 107 us
  Pallas kernels  103 us (96%)
  local copies, waits for them, and re-layouts  3.16 us (3%)
    pallas_call x1, Pallas kernels, layer(): pl.pallas_call(functools.partial(layer_kernel, ctx_size, weight is not No...  103 us
    unnamed x1, local copies, waits for them, and re-layouts  3.16 us

profile of v6, /device:TPU:1, one launch (start us, length us, event | category | flops | bytes accessed | tf_op | source)
XLA Modules:
  0.0 106.6 jit_solution(4324299358159385970)
XLA Ops:
  0.0 103.5 %layer.1 = bf16[512,2048]{1,0:T(8,128)(2,1)} custom-call(bf16[512,2048]{1,0:T(8,128)(2,1)} %refs_0_.1, bf16[512,2048]{1,0:T(8,128)(2,1)} %refs_1_.1, bf16[512,2048]{1,0:T(8,128)(2,1)} %refs_2_.1, bf16[2048,128]{1,0:T(8,128)(2,1)} %refs_3_.1), custom_call_target="tpu_custom_call" | custom-call | tf_op jit(solution)/shard_map/layer/pallas_call | solution.py:550
  103.5 3.2 %copy.6 = bf16[512,2048]{1,0:T(8,128)(2,1)} copy(bf16[512,2048]{1,0:T(8,128)(2,1)} %layer.1) | data formatting | bytes 4194304

commit v7 on v6

--- a/solution.py
+++ b/solution.py
@@ -191,7 +191,7 @@
 REACH = 7
 CHUNKS = 8
 AHEAD = 4
-WEIGHT_CHUNKS = (0, 2, 4, 3, 3, 5, 7)
+WEIGHT_CHUNKS = (0, 2, 4, 1, 3, 5, 3, 3, 5, 7)
 CHUNK_HEADS = HEADS // CHUNKS
 
 
@@ -351,29 +351,48 @@
 
         always = None
         can_go = {1: z + 1 < depth, -1: z >= 1}
+        column = (position // 2) % 2
+        rims_way = {1: column == 1, -1: column == 0}
+        at_end = {1: z == depth - 1, -1: z == 0}
+        by_z = {
+            1: (z + 1 < depth) & ((column == 0) | (z + 1 != depth - 1)),
+            -1: (z >= 1) & ((column == 1) | (z != 1)),
+        }
         first = [(always, lambda: to_x(position))]
         for way in (1, -1):
             first.append((can_go[way], functools.partial(to_z, position, way)))
         first.append((always, lambda: to_core(position, group, True)))
         first.append((always, lambda: to_core(position, 1 - group, False)))
         steps.append([(always, None, first)])
-        second = [(can_go[way], functools.partial(to_z, partner, way)) for way in (1, -1)]
+        second = [(by_z[way], functools.partial(to_z, partner, way)) for way in (1, -1)]
         second.append((always, lambda: to_y(partner)))
         second.append((always, lambda: to_core(partner, group, True)))
         steps.append([(always, (partner, group), second)])
+        late_steps = []
         for hops in range(1, depth):
-            step = []
+            step, late = [], []
             for way in (1, -1):
                 here = (z - hops * way >= 0) & (z - hops * way < depth)
                 for base in (position, partner):
                     shard = base - 4 * hops * way
+                    own = base is position
+                    onward = can_go[way] if own else by_z[way]
                     sends = [
-                        (can_go[way], functools.partial(to_z, shard, way)),
+                        (onward, functools.partial(to_z, shard, way)),
                         (always, functools.partial(to_y, shard)),
                         (always, functools.partial(to_core, shard, group, True)),
                     ]
-                    step.append((here, (shard, group), sends))
+                    over_x = at_end[way] & rims_way[way]
+                    if own:
+                        pass_x = at_end[way] & jnp.logical_not(rims_way[way])
+                        sends.append((pass_x, functools.partial(to_x, shard)))
+                        step.append((here, (shard, group), sends))
+                    else:
+                        step.append((here & jnp.logical_not(over_x), (shard, group), sends))
+                        late.append((here & over_x, (shard, group), sends[1:]))
             steps.append(step)
+            late_steps.append(late)
+        steps += late_steps
         for hops in range(depth):
             step = []
             for way in (1, -1):

time: 107 us -> 101 us (0.944)
  Pallas kernels: 103 us -> 97 us
    pallas_call x1, Pallas kernels: 103 us -> 97 us  [layer(): pl.pallas_call(functools.partial(layer_kernel, ctx_size, weight is not No...]
where the time goes in v7:
time: 101 us; the launch traced here: 100 us
  Pallas kernels  97 us (96%)
  local copies, waits for them, and re-layouts  3.16 us (3%)
    pallas_call x1, Pallas kernels, layer(): pl.pallas_call(functools.partial(layer_kernel, ctx_size, weight is not No...  97 us
    unnamed x1, local copies, waits for them, and re-layouts  3.16 us

profile of v7, /device:TPU:1, one launch (start us, length us, event | category | flops | bytes accessed | tf_op | source)
XLA Modules:
  0.0 100.2 jit_solution(13680088067965325560)
XLA Ops:
  0.0 97.0 %layer.1 = bf16[512,2048]{1,0:T(8,128)(2,1)} custom-call(bf16[512,2048]{1,0:T(8,128)(2,1)} %refs_0_.1, bf16[512,2048]{1,0:T(8,128)(2,1)} %refs_1_.1, bf16[512,2048]{1,0:T(8,128)(2,1)} %refs_2_.1, bf16[2048,128]{1,0:T(8,128)(2,1)} %refs_3_.1), custom_call_target="tpu_custom_call" | custom-call | tf_op jit(solution)/shard_map/layer/pallas_call | solution.py:569
  97.0 3.2 %copy.6 = bf16[512,2048]{1,0:T(8,128)(2,1)} copy(bf16[512,2048]{1,0:T(8,128)(2,1)} %layer.1) | data formatting | bytes 4194304
